TPU v7x, 512 devices: a whole 4x4x16 slice. The times are simulated.
512 devices in a mesh: blocks: 128 (over z, x, core), vol: 4 (over y).
Axes of the slice: x: 4, y: 4, z: 16, core: 2. Of those that a mesh axis runs over, the one named last changes fastest.
Arguments:
- features: bfloat16 [4, 1024, 16384], P('vol', 'blocks'), may hold values from -6 to 6
- active: int32 [4, 1024], P('vol', 'blocks'), may hold values 0 or 1
- coarse_grad: bfloat16 [4, 128, 32768], P('vol', 'blocks'), may hold values from -6 to 6
- conv_weight: bfloat16 [27, 32, 32], replicated, may hold values from -0.21875 to 0.21875
- down_weight: bfloat16 [8, 32, 64], replicated, may hold values from -0.375 to 0.375
Outputs:
- feature_grad: bfloat16 [4, 1024, 16384], P('vol', 'blocks')
- conv_weight_grad: float32 [27, 32, 32], replicated
- down_weight_grad: float32 [8, 32, 64], replicated
All inputs are finite; a program needn't handle non-finite values. No bound on the sum of `active` on one device may be relied on, other than what follows from the above.
Results may differ from a plain program's by a relative error of at most 0.0065.
Values may be sent and summed in bfloat16 or wider, within the bound.
No kernel may reach another device: no remote copies, remote signals or barrier semaphores. Data moves between devices by JAX's collectives and lax.ppermute only.
A program may use at most 128 MiB of HBM per device.

v0:
```python
import jax
import jax.numpy as jnp
from jax import lax
from jax.sharding import PartitionSpec as P

EDGE = 8
SIDE = 2


def extended(block, sides, width):
    for axis, dim in sides:
        count = lax.axis_size(axis)
        forward = [(i, i + 1) for i in range(count - 1)]
        backward = [(target, source) for source, target in forward]
        low = lax.ppermute(
            lax.slice_in_dim(block, block.shape[dim] - width, None, axis=dim), axis, forward
        )
        high = lax.ppermute(lax.slice_in_dim(block, 0, width, axis=dim), axis, backward)
        block = jnp.concatenate([low, block, high], axis=dim)
    return block


def to_grid(tiles, layers, side, edge, chans):
    cube = tiles.reshape(layers, side, side, edge, edge, edge, chans)
    return cube.transpose(0, 3, 1, 4, 2, 5, 6).reshape(
        layers * edge, side * edge, side * edge * chans
    )


def to_tiles(grid, layers, side, edge, chans):
    cube = grid.reshape(layers, edge, side, edge, side, edge, chans)
    return cube.transpose(0, 2, 4, 1, 3, 5, 6).reshape(layers * side * side, edge**3 * chans)


def shifters(width):
    rows = jnp.arange(width)[None, :, None]
    cols = jnp.arange(width)[None, None, :]
    offset = jnp.arange(3)[:, None, None]
    return (rows == cols + offset - 1).astype(jnp.float32)


def banded(kernel, width, chans):
    matrix = jnp.einsum("oij,zyoab->zyiajb", shifters(width), kernel.astype(jnp.float32))
    return matrix.reshape(3, 3, width * chans, width * chans).astype(jnp.bfloat16)


def forward_conv(volume, matrix, depth, width):
    padded = jnp.pad(volume, ((0, 0), (1, 1), (0, 0)))
    total = None
    for index in range(9):
        oz, oy = (index // 3, index % 3)
        term = lax.dot_general(
            padded[oz : oz + depth, oy : oy + width],
            matrix[oz, oy],
            (((2,), (0,)), ((), ())),
            preferred_element_type=jnp.float32,
        )
        total = term if total is None else total + term
    return total


def backward_conv(volume, matrix, depth, width):
    padded = jnp.pad(volume, ((0, 0), (1, 1), (0, 0)))
    total = None
    for index in range(9):
        oz, oy = (index // 3, index % 3)
        term = lax.dot_general(
            padded[2 - oz : 2 - oz + depth, 2 - oy : 2 - oy + width],
            matrix[oz, oy],
            (((2,), (1,)), ((), ())),
            preferred_element_type=jnp.float32,
        )
        total = term if total is None else total + term
    return total


def kernel_grad(volume, dpre, depth, width, chans):
    padded = jnp.pad(volume, ((0, 0), (1, 1), (0, 0)))
    shift_table = shifters(width)
    terms = []
    for index in range(9):
        oz, oy = (index // 3, index % 3)
        outer = lax.dot_general(
            padded[oz : oz + depth, oy : oy + width],
            dpre,
            (((0, 1), (0, 1)), ((), ())),
            preferred_element_type=jnp.float32,
        )
        terms.append(
            jnp.einsum("oij,iajb->oab", shift_table, outer.reshape(width, chans, width, chans))
        )
    return jnp.stack(terms).reshape(27, chans, chans)


def shards(features, active, coarse_grad, conv_weight, down_weight):
    slots = features.shape[1]
    chans = conv_weight.shape[1]
    outs = down_weight.shape[2]
    layers = slots // (SIDE * SIDE)
    depth = layers * EDGE
    width = SIDE * EDGE
    scale = 1.0 / jnp.sqrt(
        jnp.float32(lax.axis_size("vol") * lax.axis_size("blocks") * slots * EDGE**3)
    )
    live = active[0].astype(jnp.bfloat16)
    masked = features[0] * live[:, None]
    mask = jnp.broadcast_to(
        active[0].reshape(layers, 1, SIDE, 1, SIDE, 1, 1).astype(jnp.float32),
        (layers, EDGE, SIDE, EDGE, SIDE, EDGE, chans),
    ).reshape(depth, width, width * chans)
    matrix = banded(conv_weight.reshape(3, 3, 3, chans, chans), width, chans)
    coarse = to_grid(coarse_grad[0], layers // 2, SIDE // 2, EDGE, outs).reshape(
        depth // 2, width // 2, width // 2, outs
    )
    down = down_weight.reshape(2, 2, 2, chans, outs)
    wide = extended(masked, (("blocks", 0),), SIDE * SIDE)
    deep = to_grid(wide, layers + 2, SIDE, EDGE, chans)[EDGE - 1 : EDGE + depth + 1]
    grid = deep[1:-1]
    pre = forward_conv(deep, matrix, depth, width)
    sig = jax.nn.sigmoid(pre)
    ystate = (grid.astype(jnp.float32) + mask * pre * sig).astype(jnp.bfloat16)
    dy = jnp.einsum(
        "abcn,pqrmn->apbqcrm", coarse, down, preferred_element_type=jnp.float32
    ).reshape(depth, width, width * chans)
    ysix = ystate.reshape(depth // 2, 2, width // 2, 2, width // 2, 2, chans)
    down_part = jnp.einsum(
        "apbqcrm,abcn->pqrmn", ysix, coarse, preferred_element_type=jnp.float32
    ).reshape(8, chans, outs)
    dpre = (mask * dy * sig * (1.0 + pre * (1.0 - sig))).astype(jnp.bfloat16)
    dpre_tiles = to_tiles(dpre, layers, SIDE, EDGE, chans)
    dpre_wide = extended(dpre_tiles, (("blocks", 0),), SIDE * SIDE)
    dpre_deep = to_grid(dpre_wide, layers + 2, SIDE, EDGE, chans)[EDGE - 1 : EDGE + depth + 1]
    back = backward_conv(dpre_deep, matrix, depth, width)
    result = to_tiles((mask * (dy + back)).astype(jnp.bfloat16), layers, SIDE, EDGE, chans)
    conv_part = kernel_grad(deep, dpre, depth, width, chans)
    conv_total, down_total = lax.psum((conv_part, down_part), ("blocks", "vol"))
    return (result[None], conv_total * scale, down_total * scale)


def solution(mesh):
    placed = (P("vol", "blocks", None), P("vol", "blocks"), P("vol", "blocks", None), P(), P())
    return jax.shard_map(
        shards,
        mesh=mesh,
        in_specs=placed,
        out_specs=(P("vol", "blocks", None), P(), P()),
        check_vma=False,
    )
```

profile of v0, /device:TPU:1, one launch (start us, length us, event | category | flops | bytes accessed | tf_op | source)
XLA Modules:
  0.0 661.0 jit_solution(7715858454488468417)
XLA Ops:
  9.0 4.5 collective-permute-start
  13.5 5.6 collective-permute-start.1
  20.5 9.7 %convert_bitcast_fusion = bf16[3,3,16,32,16,32]{5,4,3,1,0,2:T(8,128)(2,1)} fusion(bf16[3,3,3,32,32]{4,3,2,1,0:T(8,128)(2,1)} %bitcast.279, s32[3,16]{1,0:T(4,128)S(1)} %add_add_fusion), kind=kOutput, calls=%fused_computation | convolution fusion | flops 16515840 | bytes 4774080 | tf_op jit(solution)/shard_map/oij,zyoab->zyiajb/dot_general | solution.py:43
  32.8 17.8 %copy.23 = bf16[3,3,16,32,16,32]{5,4,3,2,1,0:T(8,128)(2,1)} copy(bf16[3,3,16,32,16,32]{5,4,3,1,0,2:T(8,128)(2,1)} %convert_bitcast_fusion) | data formatting | bytes 9437184 | tf_op jit(solution)/shard_map/convert_element_type | solution.py:44
  50.6 25.2 %convert_element_type.55 = bf16[3,3,512,512]{3,2,1,0:T(8,128)(2,1)} reshape(bf16[3,3,16,32,16,32]{5,4,3,2,1,0:T(8,128)(2,1)} %copy.23) | data formatting | bytes 9437184 | tf_op jit(solution)/shard_map/convert_element_type | solution.py:44
  75.8 3.2 copy.20
  79.0 3.5 reshape.113
  84.7 2.6 reshape.114
  89.3 2.5 reshape.115
  91.9 2.3 fusion.36
  96.4 2.1 fusion.40
  98.5 2.1 fusion.44
  103.2 2.3 fusion.48
  110.0 2.3 add_convert_fusion
  121.9 2.7 reshape.122
  125.7 3.7 reshape.123
  129.4 2.2 reshape.124
  131.6 2.2 reshape.125
  137.1 2.2 reshape.126
  139.3 2.2 reshape.127
  141.4 2.2 reshape.128
  143.6 2.9 reshape.129
  146.5 2.8 fusion.30
  149.3 2.8 fusion.29
  165.4 2.4 collective-permute-start.3
  167.8 454.4 %all-reduce.5.cloned.1.call-done = (f32[27,32,32]{2,1,0:T(8,128)}, f32[8,32,64]{2,1,0:T(8,128)}) async-done(((f32[27,32,32]{2,1,0:T(8,128)}, f32[8,32,64]{2,1,0:T(8,128)}), (f32[27,32,32]{2,1,0:T(8,128)}, f32[8,32,64]{2,1,0:T(8,128)})) %all-reduce.5.cloned.1.call-update) | async-done | bytes 176144 | tf_op jit(solution)/shard_map/psum | solution.py:136
  629.5 3.4 reshape.120
  634.2 2.2 fusion.37
  636.4 2.2 fusion.39
  638.7 2.2 fusion.43
  640.8 2.2 fusion.45
  643.0 2.2 fusion.47
  (134 shorter events, 63.4 us)
Async XLA Ops:
  7.2 23.1 %copy-start = (bf16[8,32,64]{2,1,0:T(8,128)(2,1)S(1)}, bf16[8,32,64]{2,1,0:T(8,128)(2,1)}, u32[]{:S(2)}) copy-start(bf16[8,32,64]{2,1,0:T(8,128)(2,1)} %param.9) | copy-start | bytes 98308
  7.2 615.0 %all-reduce.5.cloned.1.call-start = ((), (), s32[]{:S(2)}) async-start(), calls=%async_computation | async-start | bytes 1146880 | tf_op jit(solution)/shard_map/psum | solution.py:136
  9.0 75.5 %collective-permute-start = (bf16[4,16384]{1,0:T(4,128)(2,1)S(1)}, bf16[4,16384]{1,0:T(4,128)(2,1)S(1)}, u32[]{:S(2)}, u32[]{:S(2)}) collective-permute-start(bf16[4,16384]{1,0:T(4,128)(2,1)S(1)} %get-tuple-element.9), channel_id=1, source_target_pairs={{0,4},{4,8},{8,12},{12,16},{16,20},{20,24},{24,28},{28,32},{32,36}... | collective-permute-start | bytes 393224 | tf_op jit(solution)/shard_map/ppermute | solution.py:15
  13.5 70.9 %collective-permute-start.1 = (bf16[4,16384]{1,0:T(4,128)(2,1)S(1)}, bf16[4,16384]{1,0:T(4,128)(2,1)S(1)}, u32[]{:S(2)}, u32[]{:S(2)}) collective-permute-start(bf16[4,16384]{1,0:T(4,128)(2,1)S(1)} %get-tuple-element.10), channel_id=1, source_target_pairs={{4,0},{8,4},{12,8},{16,12},{20,16},{24,20},{28,24},{32,28},{36,32}... | collective-permute-start | bytes 393224 | tf_op jit(solution)/shard_map/ppermute | solution.py:18
  79.0 3.5 copy-start.30
  91.9 6.7 %copy-start.10 = (bf16[32,16,512]{2,1,0:T(8,128)(2,1)}, bf16[32,16,512]{2,1,0:T(8,128)(2,1)S(1)}, u32[]{:S(2)}) copy-start(bf16[32,16,512]{2,1,0:T(8,128)(2,1)S(1)} %reshape.115) | copy-start | bytes 1572868
  103.1 4.8 copy-start.11
  103.1 4.8 copy-start.18
  103.2 4.8 copy-start.19
  106.4 3.5 copy-start.8
  107.9 2.0 copy-start.12
  107.9 2.0 copy-start.14
  107.9 2.0 copy-start.27
  125.7 3.7 copy-start.26
  125.7 5.9 copy-start.25
  131.6 3.8 copy-start.9
  131.6 5.4 copy-start.24
  135.5 3.8 copy-start.23
  137.1 4.4 copy-start.22
  146.4 5.6 copy-start.5
  149.3 3.9 copy-start.6
  149.3 3.9 copy-start.7
  153.2 1.8 copy-start.4
  154.3 1.7 copy-start.3
  162.9 462.7 %collective-permute-start.2 = (bf16[4,16384]{1,0:T(4,128)(2,1)S(1)}, bf16[4,16384]{1,0:T(4,128)(2,1)S(1)}, u32[]{:S(2)}, u32[]{:S(2)}) collective-permute-start(bf16[4,16384]{1,0:T(4,128)(2,1)S(1)} %slice.167), channel_id=1, source_target_pairs={{0,4},{4,8},{8,12},{12,16},{16,20},{20,24},{24,28},{28,32},{32,36}... | collective-permute-start | bytes 393224 | tf_op jit(solution)/shard_map/ppermute | solution.py:15
  165.4 460.2 %collective-permute-start.3 = (bf16[4,16384]{1,0:T(4,128)(2,1)S(1)}, bf16[4,16384]{1,0:T(4,128)(2,1)S(1)}, u32[]{:S(2)}, u32[]{:S(2)}) collective-permute-start(bf16[4,16384]{1,0:T(4,128)(2,1)S(1)} %slice.169), channel_id=1, source_target_pairs={{4,0},{8,4},{12,8},{16,12},{20,16},{24,20},{28,24},{32,28},{36,32}... | collective-permute-start | bytes 393224 | tf_op jit(solution)/shard_map/ppermute | solution.py:18
  645.2 2.6 copy-start.16
  645.2 2.6 copy-start.17
  647.8 1.9 copy-start.13
  647.9 1.9 copy-start.15
  647.9 1.9 copy-start.20
  649.8 4.2 copy-start.1
  (4 other events, 5.0 us)
Sparse Core Ops, SparseCore 0:
  161.3 460.8 all-reduce.4
where the time goes:
time: 671 us; the launch traced here: 661 us
  waiting for transfers between devices  454 us (68%)
  local copies, waits for them, and re-layouts  102 us (15%)
  matrix products  68.9 us (10%)
  between operations  14.8 us (2%)
  starting transfers between devices  14.5 us (2%)
  other arithmetic  6.86 us (1%)
    psum x1, waiting for transfers between devices, shards(): conv_total, down_total = lax.psum((conv_part, down_part), ('blocks', 'vol'))  454 us
    convert_element_type x2, local copies, waits for them, and re-layouts, banded(): matrix.reshape(3, 3, width * chans, width * chans).astype(jnp.bfloat16)  43 us
    reshape x8, local copies, waits for them, and re-layouts, kernel_grad(): outer.reshape(width, chans, width, chans)  20.2 us
    dot_general x9, matrix products, forward_conv(): lax.dot_general(padded[oz:oz + depth, oy:oy + width], matrix[oz, oy], (((...  18.9 us
    dot_general x9, matrix products, backward_conv(): lax.dot_general(padded[2 - oz:2 - oz + depth, 2 - oy:2 - oy + width], mat...  17 us
  transfers between devices with their start and end apart: 5, of which 1 were waited for; matrix products, arithmetic and copies ran while one was open for 11% of the time, Pallas kernels for 0%

commit v1 on v0

v1 whole, which is shorter than its diff:
```python
import jax
import jax.numpy as jnp
from jax import lax
from jax.experimental import pallas as pl
from jax.experimental.pallas import tpu as pltpu
from jax.sharding import Mesh
from jax.sharding import PartitionSpec as P

BLOCKS = ("z", "x", "core")
NEAR = ("x", "core", "vol")
F32 = jnp.float32
BF16 = jnp.bfloat16

ROW = 256
WIDE = 384
PIECE = 16


def iota(shape, dim):
    return lax.broadcasted_iota(jnp.int32, shape, dim)


def live_rows(active_ref, lanes):
    slot = iota((8, lanes), 0)
    out = jnp.zeros((8, lanes), F32)
    for b in range(8):
        out = jnp.where(slot == b, active_ref[0, b].astype(F32), out)
    return out


def repeat_lanes(rows, lanes):
    return (iota((rows, lanes), 1) % rows == iota((rows, lanes), 0)).astype(BF16)


def widen(row):
    slot, lane = iota((8, 128), 0), iota((8, 128), 1)
    right = pltpu.roll(row[:, :128], 7, 0)
    left = pltpu.roll(row[:, 128:], 1, 0)
    edge = jnp.where(
        (slot % 2 == 0) & (lane < 32), right, jnp.where((slot % 2 == 1) & (lane >= 96), left, 0.0)
    )
    return jnp.concatenate([row, edge], axis=1)


def put_plane(outer, inner, z, rows):
    full = [widen(row) for row in rows]
    upper = (iota((8, WIDE), 0) // 2) % 2
    low = jnp.where(upper == 1, pltpu.roll(full[7], 2, 0), 0.0)
    high = jnp.where(upper == 0, pltpu.roll(full[0], 6, 0), 0.0)
    ring = [low] + full + [high]
    for k in range(5):
        outer[z, 16 * k : 16 * k + 16] = jnp.concatenate(ring[2 * k : 2 * k + 2], 0).astype(BF16)
    for k in range(4):
        inner[z, 16 * k : 16 * k + 16] = jnp.concatenate(full[2 * k : 2 * k + 2], 0).astype(BF16)


def window(outer, inner, first, count, oz, oy):
    source = inner if oy == 1 else outer
    start = 16 if oy == 2 else 0
    return source[first + oz : first + oz + count, start : start + 64, :].reshape(count * 64, WIDE)


def put_bands(bands, index, taps):
    spot = iota((32, ROW), 1) // 32
    for i in range(8):
        part = jnp.zeros((32, ROW), F32)
        for ox in range(3):
            part = jnp.where(spot == i + 1 - ox, taps[ox], part)
        bands[index, 32 * i : 32 * i + 32] = part.astype(BF16)
    bands[index, 256:288] = jnp.where(spot == 7, taps[2], 0.0).astype(BF16)
    bands[index, 288:352] = jnp.zeros((64, ROW), BF16)
    bands[index, 352:384] = jnp.where(spot == 0, taps[0], 0.0).astype(BF16)


def pack_kernel(active, features, coarse, to_next, to_prev, coarse_rows):
    live = live_rows(active, ROW)
    slot = iota((8, ROW), 0)
    row, col = iota((128, 128), 0), iota((128, 128), 1)
    zc, yc, b = row // 32, (row // 8) % 4, row % 8
    source = (((b // 4) * 4 + zc) * 8 + ((b // 2) % 2) * 4 + yc) * 2 + b % 2
    kept = jnp.concatenate([live[:, :128]] * 16, axis=0)
    pick = jnp.where(source == col, kept, 0.0).astype(BF16)
    rows = jnp.dot(pick, coarse[...], preferred_element_type=F32)
    coarse_rows[...] = rows.astype(BF16)

    def fine(z, y):
        start = (z * 8 + y) * ROW
        return features[:, start : start + ROW].astype(F32) * live

    for y in range(8):
        lanes = slice(y * ROW, y * ROW + ROW)
        to_next[:, lanes] = jnp.where(slot < 4, pltpu.roll(fine(6, y), 4, 0), fine(7, y)).astype(BF16)
        to_prev[:, lanes] = jnp.where(slot < 4, fine(1, y), pltpu.roll(fine(0, y), 4, 0)).astype(BF16)
    for k in range(2):
        lanes = slice(2048 + k * ROW, 2048 + k * ROW + ROW)
        last = [rows[96 + 8 * y : 104 + 8 * y] for y in (2 * k, 2 * k + 1)]
        first = [rows[8 * y : 8 * y + 8] for y in (2 * k, 2 * k + 1)]
        to_next[:, lanes] = jnp.where(slot < 4, pltpu.roll(last[0], 4, 0), last[1]).astype(BF16)
        to_prev[:, lanes] = jnp.where(slot < 4, first[1], pltpu.roll(first[0], 4, 0)).astype(BF16)


def inner_kernel(active, features, conv, down, outer, inner, bands, spread):
    live = live_rows(active, ROW)
    for z in range(8):
        rows = []
        for y in range(8):
            start = (z * 8 + y) * ROW
            rows.append(features[:, start : start + ROW].astype(F32) * live)
        put_plane(outer, inner, z, rows)
    tile = repeat_lanes(32, ROW)
    taps = jnp.dot(conv[...].reshape(27 * 32, 32), tile, preferred_element_type=F32)
    for index in range(9):
        put_bands(bands, index, [taps[96 * index + 32 * ox : 96 * index + 32 * ox + 32] for ox in range(3)])
    spot = iota((64, ROW), 1) // 32
    for q in range(4):
        turned = [
            lax.dot_general(down[2 * q + ox], tile, (((0,), (0,)), ((), ())), preferred_element_type=F32)
            for ox in range(2)
        ]
        for cx in range(4):
            part = jnp.where(spot == 2 * cx, turned[0], jnp.where(spot == 2 * cx + 1, turned[1], 0.0))
            spread[64 * cx : 64 * cx + 64, ROW * q : ROW * q + ROW] = part.astype(BF16)


def main_kernel(
    scale, inner_own, outer_own, from_prev, from_next, coarse_rows, bands, spread,
    grads, dpre, dy, outer, inner, coarse, pre, spread_out, state,
):
    slot = iota((8, ROW), 0)
    outer[2:10] = outer_own[...]
    inner[2:10] = inner_own[...]

    def own(z, y):
        return inner_own[z, 16 * (y // 2) : 16 * (y // 2) + 16, :ROW].astype(F32)[8 * (y % 2) : 8 * (y % 2) + 8]

    before, beyond, after, past = [], [], [], []
    for y in range(8):
        low = from_prev[:, y * ROW : y * ROW + ROW].astype(F32)
        high = from_next[:, y * ROW : y * ROW + ROW].astype(F32)
        beyond.append(jnp.where(slot < 4, low, pltpu.roll(own(6, y), 4, 0)))
        before.append(pltpu.roll(jnp.where(slot >= 4, low, own(7, y)), 4, 0))
        after.append(jnp.where(slot >= 4, high, pltpu.roll(own(0, y), 4, 0)))
        past.append(pltpu.roll(jnp.where(slot < 4, high, own(1, y)), 4, 0))
    for z, rows in ((0, beyond), (1, before), (10, after), (11, past)):
        put_plane(outer, inner, z, rows)

    coarse[32:160] = coarse_rows[...]
    for k in range(2):
        lanes = slice(2048 + k * ROW, 2048 + k * ROW + ROW)
        low, high = from_prev[:, lanes].astype(F32), from_next[:, lanes].astype(F32)
        last = coarse_rows[96 + 16 * k : 112 + 16 * k].astype(F32)
        first = coarse_rows[16 * k : 16 * k + 16].astype(F32)
        under = [
            jnp.where(slot < 4, low, pltpu.roll(last[:8], 4, 0)),
            pltpu.roll(jnp.where(slot >= 4, low, last[8:]), 4, 0),
        ]
        over = [
            jnp.where(slot >= 4, high, pltpu.roll(first[:8], 4, 0)),
            pltpu.roll(jnp.where(slot < 4, high, first[8:]), 4, 0),
        ]
        coarse[16 * k : 16 * k + 16] = jnp.concatenate(under, 0).astype(BF16)
        coarse[160 + 16 * k : 176 + 16 * k] = jnp.concatenate(over, 0).astype(BF16)

    spread_out[...] = jnp.dot(coarse[...], spread[...], preferred_element_type=F32)
    total = None
    for oz in range(3):
        for oy in range(3):
            term = jnp.dot(
                window(outer, inner, 0, 10, oz, oy), bands[3 * oz + oy], preferred_element_type=F32
            )
            total = term if total is None else total + term
    pre[...] = total

    for step in range(10):
        z = step - 1
        zc, qz = z // 2 + 1, z % 2
        slope = []
        for pair in range(4):
            rows = slice(64 * step + 16 * pair, 64 * step + 16 * pair + 16)
            u = pre[rows]
            sig = 0.5 * jnp.tanh(0.5 * u) + 0.5
            silu = u * sig
            base = 32 * zc + 8 * pair
            back = jnp.concatenate(
                [spread_out[base : base + 8, ROW * (2 * qz + qy) : ROW * (2 * qz + qy) + ROW] for qy in range(2)], 0
            )
            dpre[step, 16 * pair : 16 * pair + 16] = (back * sig * (1.0 + (u - silu))).astype(BF16)
            if 0 <= z < 8:
                dy[z, 16 * pair : 16 * pair + 16] = back
                slope.append(inner[z + 2, 16 * pair : 16 * pair + 16, :ROW].astype(F32) + silu)
        if 0 <= z < 8:
            for qy in range(2):
                for half in range(2):
                    y = jnp.concatenate(
                        [slope[2 * half + k][8 * qy : 8 * qy + 8] for k in range(2)], 0
                    )
                    start = 32 * (z // 2) + 16 * half
                    state[2 * qz + qy, start : start + 16] = y.astype(BF16)

    lane = iota((32, 128), 1)
    turned = dpre[1:9].reshape(512, ROW).astype(F32).T.astype(BF16)
    for index in range(9):
        outer_sum = jnp.dot(
            turned, window(outer, inner, 1, 8, index // 3, index % 3), preferred_element_type=F32
        )
        block = [outer_sum[32 * j : 32 * j + 32] for j in range(8)]
        v0, v1, edge = slice(0, 128), slice(128, 256), slice(256, 384)
        t0 = jnp.where(lane >= 96, block[0][:, edge] + block[4][:, v0], block[0][:, v0] + block[4][:, v1])
        t1 = block[1][:, v0] + block[5][:, v1]
        t2 = block[2][:, v0] + block[6][:, v1]
        t3 = jnp.where(lane < 32, block[3][:, v1] + block[7][:, edge], block[3][:, v0] + block[7][:, v1])
        folded = pltpu.roll(t0, 32, 1) + t1 + pltpu.roll(t2, 96, 1) + pltpu.roll(t3, 64, 1)
        grads[32 * index : 32 * index + 32] = jnp.where(lane < 96, folded * scale, 0.0)
    own_coarse = coarse[32:160]
    for q in range(4):
        outer_sum = lax.dot_general(
            state[q], own_coarse, (((0,), (0,)), ((), ())), preferred_element_type=F32
        )
        block = [outer_sum[32 * x : 32 * x + 32] for x in range(8)]
        even = [block[qx][:, :128] + block[4 + qx][:, 128:] for qx in range(2)]
        odd = [block[2 + qx][:, :128] + block[6 + qx][:, 128:] for qx in range(2)]
        folded = jnp.where(lane < 64, even[0], odd[1]) + pltpu.roll(
            jnp.where(lane < 64, even[1], odd[0]), 64, 1
        )
        grads[288 + 32 * q : 320 + 32 * q] = folded * scale
    grads[416:512] = jnp.zeros((96, 128), F32)


def back_kernel(active, conv, dpre, dy, result, outer, inner, bands):
    live = live_rows(active, ROW)
    tile = repeat_lanes(32, ROW)
    for index in range(9):
        taps = [
            lax.dot_general(
                conv[26 - (3 * index + ox)], tile, (((0,), (0,)), ((), ())), preferred_element_type=F32
            )
            for ox in range(3)
        ]
        put_bands(bands, index, taps)
    for z in range(10):
        rows = []
        for pair in range(4):
            both = dpre[z, 16 * pair : 16 * pair + 16].astype(F32)
            rows += [both[:8], both[8:]]
        put_plane(outer, inner, z, rows)
    total = None
    for oz in range(3):
        for oy in range(3):
            term = jnp.dot(
                window(outer, inner, 0, 8, oz, oy), bands[3 * oz + oy], preferred_element_type=F32
            )
            total = term if total is None else total + term
    for z in range(8):
        for y in range(8):
            row = 64 * z + 8 * y
            value = dy[z, 8 * y : 8 * y + 8] + live * total[row : row + 8]
            result[:, row * 32 : row * 32 + ROW] = value.astype(BF16)


def sum_kernel(parts, out):
    total = parts[0]
    for k in range(1, parts.shape[0]):
        total = total + parts[k]
    for k in range(out.shape[0]):
        out[k] = total.astype(out.dtype)


def finish_kernel(whole, conv_grad, down_grad):
    def rows(start, count):
        parts = []
        for piece in range(start // PIECE, (start + count) // PIECE):
            parts.append(whole[piece].astype(F32))
        return jnp.concatenate(parts, 0)

    for index in range(9):
        turned = rows(32 * index, 32).T
        for ox in range(3):
            conv_grad[3 * index + ox] = turned[32 * ox : 32 * ox + 32]
    for q in range(4):
        both = rows(288 + 32 * q, 32)
        down_grad[2 * q] = both[:, :64]
        down_grad[2 * q + 1] = pltpu.roll(both, 64, 1)[:, :64]


def call(kernel, outs, scalars, arrays, scratch=(), name=None):
    spaces = [pltpu.SMEM] * len(scalars) + [pltpu.VMEM] * len(arrays)
    return pl.pallas_call(
        kernel,
        out_shape=[jax.ShapeDtypeStruct(shape, dtype) for shape, dtype in outs],
        in_specs=[pl.BlockSpec(memory_space=space) for space in spaces],
        out_specs=[pl.BlockSpec(memory_space=pltpu.VMEM)] * len(outs),
        scratch_shapes=[pltpu.VMEM(shape, dtype) for shape, dtype in scratch],
        compiler_params=pltpu.CompilerParams(vmem_limit_bytes=40 * 2**20),
        name=name,
    )(*scalars, *arrays)


def shards(features, active, coarse_grad, conv_weight, down_weight):
    fine = features[0]
    devices = lax.axis_size(BLOCKS)
    scale = (lax.axis_size("vol") * devices * fine.size // 32) ** -0.5
    to_next, to_prev, coarse_rows = call(
        pack_kernel,
        [((8, 2560), BF16), ((8, 2560), BF16), ((128, ROW), BF16)],
        [active], [fine, coarse_grad.reshape(128, ROW)], name="pack",
    )
    up = [(i, i + 1) for i in range(devices - 1)]
    from_prev = lax.ppermute(to_next, BLOCKS, up)
    from_next = lax.ppermute(to_prev, BLOCKS, [(j, i) for i, j in up])
    outer, inner, bands, spread = call(
        inner_kernel,
        [((8, 80, WIDE), BF16), ((8, 64, WIDE), BF16), ((9, WIDE, ROW), BF16), ((ROW, 4 * ROW), BF16)],
        [active], [fine, conv_weight, down_weight], name="inner",
    )
    grads, dpre, dy = call(
        lambda *refs: main_kernel(scale, *refs),
        [((512, 128), F32), ((10, 64, ROW), BF16), ((8, 64, ROW), F32)],
        [], [inner, outer, from_prev, from_next, coarse_rows, bands, spread],
        [
            ((12, 80, WIDE), BF16), ((12, 64, WIDE), BF16), ((192, ROW), BF16),
            ((640, ROW), F32), ((192, 4 * ROW), F32), ((4, 128, ROW), BF16),
        ],
        name="main",
    )
    count, far = lax.axis_size(NEAR), lax.axis_size("z")
    pieces = 512 // PIECE
    cut = grads.reshape(count, pieces // count, PIECE, 128) if count != pieces else grads.reshape(count, PIECE, 128)
    cut = lax.all_to_all(cut, NEAR, 0, 0)
    (result,) = call(
        back_kernel, [((8, 64 * ROW), BF16)],
        [active], [conv_weight, dpre, dy],
        [((10, 80, WIDE), BF16), ((10, 64, WIDE), BF16), ((9, WIDE, ROW), BF16)],
        name="back",
    )
    (mine,) = call(sum_kernel, [((far,) + cut.shape[1:], F32)], [], [cut], name="sum_near")
    mine = lax.all_to_all(mine, "z", 0, 0)
    (mine,) = call(sum_kernel, [(cut.shape, F32)], [], [mine], name="sum_far")
    whole = lax.all_to_all(mine, NEAR, 0, 0).reshape(pieces, PIECE, 128)
    conv_grad, down_grad = call(
        finish_kernel, [((27, 32, 32), F32), ((8, 32, 64), F32)], [], [whole], name="finish"
    )
    return result[None], conv_grad, down_grad


def solution(mesh):
    fine = Mesh(mesh.devices.reshape(-1, 4, 2, mesh.shape["vol"]), BLOCKS + ("vol",))
    placed = (P("vol", BLOCKS, None), P("vol", BLOCKS), P("vol", BLOCKS, None), P(), P())
    return jax.shard_map(
        shards,
        mesh=fine,
        in_specs=placed,
        out_specs=(P("vol", BLOCKS, None), P(), P()),
        check_vma=False,
    )
```

time: 671 us -> 83.3 us (0.12); the launches traced: 661 us -> 82.9 us
  waiting for transfers between devices: 454 us -> 5.91 us
  local copies, waits for them, and re-layouts: 102 us -> 3.4 us
  matrix products: 68.9 us -> 0 us
  blocking collectives: 0 us -> 41.5 us
  between operations: 14.8 us -> 0.74 us
  Pallas kernels: 0 us -> 12.8 us
    psum x1 -> x0, waiting for transfers between devices: 454 us -> none  [shards(): conv_total, down_total = lax.psum((conv_part, down_part), ('blocks', 'vol'))]
    dot_general x39 -> x0, matrix products: 68.9 us -> none  [the longest x9 18.9 us: forward_conv(): lax.dot_general(padded[oz:oz + depth, oy:oy + width], matrix[oz, oy], (((...]
    convert_element_type x3 -> x0, local copies, waits for them, and re-layouts: 43.1 us -> none  [the longest x2 43 us: banded(): matrix.reshape(3, 3, width * chans, width * chans).astype(jnp.bfloat16)]
    all_to_all x0 -> x2, blocking collectives: none -> 41.5 us  [the longest x1 26.6 us: shards(): mine = lax.all_to_all(mine, 'z', 0, 0)]
    reshape x20 -> x1, local copies, waits for them, and re-layouts: 40.7 us -> 0.03 us  [shards(): coarse_grad.reshape(128, ROW)]
    pallas_call x0 -> x7, Pallas kernels: none -> 12.8 us  [call(): pl.pallas_call(kernel, out_shape=[jax.ShapeDtypeStruct(shape, dtype) for...]
    all_to_all x0 -> x1, starting transfers between devices: none -> 7.25 us  [shards(): whole = lax.all_to_all(mine, NEAR, 0, 0).reshape(pieces, PIECE, 128)]
    ppermute x4 -> x2, starting transfers between devices: 14.4 us -> 10.1 us  [the longest x1 5.57 us: shards(): from_next = lax.ppermute(to_prev, BLOCKS, [(j, i) for i, j in up])]
  transfers between devices with their start and end apart: 5 -> 3, of which waited for: 1 -> 1; matrix products, arithmetic and copies ran while one was open for 11% -> 0% of each run, Pallas kernels for 0% -> 5%
where the time goes in v1:
time: 83.3 us; the launch traced here: 82.9 us
  blocking collectives  41.5 us (50%)
  starting transfers between devices  17.3 us (21%)
  Pallas kernels  12.8 us (15%)
  waiting for transfers between devices  5.91 us (7%)
  local copies, waits for them, and re-layouts  3.4 us (4%)
  other arithmetic  1.26 us (2%)
    all_to_all x1, blocking collectives, shards(): mine = lax.all_to_all(mine, 'z', 0, 0)  26.6 us
    all_to_all x1, blocking collectives, shards(): cut = lax.all_to_all(cut, NEAR, 0, 0)  14.9 us
    pallas_call x7, Pallas kernels, call(): pl.pallas_call(kernel, out_shape=[jax.ShapeDtypeStruct(shape, dtype) for...  12.8 us
    all_to_all x1, starting transfers between devices, shards(): whole = lax.all_to_all(mine, NEAR, 0, 0).reshape(pieces, PIECE, 128)  7.25 us
    all_to_all x1, waiting for transfers between devices, shards(): whole = lax.all_to_all(mine, NEAR, 0, 0).reshape(pieces, PIECE, 128)  5.91 us
    ppermute x1, starting transfers between devices, shards(): from_next = lax.ppermute(to_prev, BLOCKS, [(j, i) for i, j in up])  5.57 us
    ppermute x1, starting transfers between devices, shards(): from_prev = lax.ppermute(to_next, BLOCKS, up)  4.51 us
    unnamed x12, local copies, waits for them, and re-layouts  3.38 us
  transfers between devices with their start and end apart: 3, of which 1 were waited for; matrix products, arithmetic and copies ran while one was open for 0% of the time, Pallas kernels for 5%

profile of v1, /device:TPU:1, one launch (start us, length us, event | category | flops | bytes accessed | tf_op | source)
XLA Modules:
  0.0 82.9 jit_solution(1651546547531340360)
XLA Ops:
  0.6 1.3 %reduce = bf16[32768]{0:T(1024)(128)(2,1)S(1)} reduce(bf16[1,1,32768]{2,1,0:T(2,128)(2,1)} %param.7, bf16[]{:T(256)} %constant.3), dimensions={0,1}, to_apply=%param.7.reduce_sub_computation | reduce | bytes 131074 | tf_op args[2]
  1.9 0.0 copy-start
  1.9 0.9 %copy-done = bf16[1,8,16384]{2,1,0:T(8,128)(2,1)S(1)} copy-done((bf16[1,8,16384]{2,1,0:T(8,128)(2,1)S(1)}, bf16[1,8,16384]{2,1,0:T(8,128)(2,1)}, u32[]{:S(2)}) %copy-start) | copy-done | bytes 262168
  2.9 0.0 copy-start.4
  2.9 0.7 copy-done.4
  3.5 0.7 pack.1
  4.3 4.5 %collective-permute-start = (bf16[8,2560]{1,0:T(8,128)(2,1)S(1)}, bf16[8,2560]{1,0:T(8,128)(2,1)S(1)}, u32[]{:S(2)}, u32[]{:S(2)}) collective-permute-start(bf16[8,2560]{1,0:T(8,128)(2,1)S(1)} %get-tuple-element.17), channel_id=1, source_target_pairs={{0,4},{4,8},{8,12},{12,16},{16,20},{20,24},{24,28},{28,32},{32,36}... | collective-permute-start | bytes 122888 | tf_op jit(solution)/shard_map/ppermute | solution.py:308
  8.8 5.6 %collective-permute-start.1 = (bf16[8,2560]{1,0:T(8,128)(2,1)S(1)}, bf16[8,2560]{1,0:T(8,128)(2,1)S(1)}, u32[]{:S(2)}, u32[]{:S(2)}) collective-permute-start(bf16[8,2560]{1,0:T(8,128)(2,1)S(1)} %get-tuple-element.18), channel_id=1, source_target_pairs={{4,0},{8,4},{12,8},{16,12},{20,16},{24,20},{28,24},{32,28},{36,32}... | collective-permute-start | bytes 122888 | tf_op jit(solution)/shard_map/ppermute | solution.py:309
  14.4 0.0 copy-start.1
  14.4 0.9 %copy-done.1 = bf16[27,32,32]{2,1,0:T(8,128)(2,1)S(1)} copy-done((bf16[27,32,32]{2,1,0:T(8,128)(2,1)S(1)}, bf16[27,32,32]{2,1,0:T(8,128)(2,1)}, u32[]{:S(2)}) %copy-start.1) | copy-done | bytes 55320
  15.3 0.0 copy-start.3
  15.3 0.8 %copy-done.3 = bf16[8,32,64]{2,1,0:T(8,128)(2,1)S(1)} copy-done((bf16[8,32,64]{2,1,0:T(8,128)(2,1)S(1)}, bf16[8,32,64]{2,1,0:T(8,128)(2,1)}, u32[]{:S(2)}) %copy-start.3) | copy-done | bytes 32792
  16.2 1.2 %inner.1 = (bf16[8,80,384]{2,1,0:T(8,128)(2,1)S(1)}, bf16[8,64,384]{2,1,0:T(8,128)(2,1)S(1)}, bf16[9,384,256]{2,1,0:T(8,128)(2,1)S(1)}, bf16[256,1024]{1,0:T(8,128)(2,1)S(1)}) custom-call(s32[1,8]{1,0:T(1,128)S(1)} %copy-done.4, bf16[8,16384]{1,0:T(8,128)(2,1)S(1)} %bitcast.4, bf16[27,32,32]{2,1,0:T(8,128)(2,1)S(1)} %copy-done.1, ...), custom_call_target="tpu_custom_call" | custom-call | tf_op jit(solution)/shard_map/inner/pallas_call | solution.py:287
  17.3 0.0 collective-permute-done.refs_2_
  17.3 0.0 collective-permute-done.1.refs_3_
  17.3 6.1 %main.1 = (f32[512,128]{1,0:T(8,128)S(1)}, bf16[10,64,256]{2,1,0:T(8,128)(2,1)S(1)}, f32[8,64,256]{2,1,0:T(8,128)S(1)}) custom-call(bf16[8,64,384]{2,1,0:T(8,128)(2,1)S(1)} %get-tuple-element.15.refs_0_, bf16[8,80,384]{2,1,0:T(8,128)(2,1)S(1)} %get-tuple-element.16.refs_1_, bf16[8,2560]{1,0:T(8,128)(2,1)S(1)} %collective-permute-done.refs_2_, ...), custom_call_target="tpu_custom_call" | custom-call | tf_op jit(solution)/shard_map/main/pallas_call | solution.py:287
  23.4 0.0 copy-start.2
  23.5 0.0 copy-start.5
  23.5 14.9 %all_to_all.15.parts = f32[32,16,128]{2,1,0:T(8,128)S(1)} all-to-all(f32[32,16,128]{2,1,0:T(8,128)S(1)} %bitcast.5), channel_id=1, replica_groups=mesh['z'=16,'x'=4,'core'=2,'vol'=4] {'x','core','vol'}, dimensions={0} | all-to-all | bytes 524288 | tf_op jit(solution)/shard_map/all_to_all | solution.py:328
  38.4 26.6 %all_to_all.16.parts = f32[16,16,128]{2,1,0:T(8,128)S(1)} all-to-all(f32[16,16,128]{2,1,0:T(8,128)S(1)} %sum_near.1), channel_id=1, replica_groups=mesh['z'=16,'x'=4,'core'=2,'vol'=4] {'z'}, dimensions={0} | all-to-all | bytes 262144 | tf_op jit(solution)/shard_map/all_to_all | solution.py:336
  65.0 0.7 sum_far.1
  65.7 7.3 %all-to-all-start.2 = ((f32[32,16,128]{2,1,0:T(8,128)}), f32[32,16,128]{2,1,0:T(8,128)S(1)}, u32[]{:S(2)}, u32[]{:S(2)}) async-start(f32[32,16,128]{2,1,0:T(8,128)} %sum_far.1), calls=%async_computation.2 | async-start | bytes 524288 | tf_op jit(solution)/shard_map/all_to_all | solution.py:338
  73.0 0.0 copy-done.2
  73.0 0.0 copy-done.5
  73.0 3.0 %back.1 = bf16[8,16384]{1,0:T(8,128)(2,1)} custom-call(s32[1,8]{1,0:T(1,128)S(1)} %copy-done.5, bf16[27,32,32]{2,1,0:T(8,128)(2,1)S(1)} %copy-done.2, bf16[10,64,256]{2,1,0:T(8,128)(2,1)S(1)} %get-tuple-element.22.dpre, f32[8,64,256]{2,1,0:T(8,128)S(1)} %get-tuple-element.23.dy), custom_call_target="tpu_custom_call" | custom-call | tf_op jit(solution)/shard_map/back/pallas_call | solution.py:287
  76.0 5.9 %all-to-all-done.2.whole = f32[32,16,128]{2,1,0:T(8,128)S(1)} async-done(((f32[32,16,128]{2,1,0:T(8,128)}), f32[32,16,128]{2,1,0:T(8,128)S(1)}, u32[]{:S(2)}, u32[]{:S(2)}) %all-to-all-start.2) | async-done | bytes 262176 | tf_op jit(solution)/shard_map/all_to_all | solution.py:338
  81.9 1.0 %finish.1 = (f32[27,32,32]{2,1,0:T(8,128)}, f32[8,32,64]{2,1,0:T(8,128)}) custom-call(f32[32,16,128]{2,1,0:T(8,128)S(1)} %all-to-all-done.2.whole), custom_call_target="tpu_custom_call" | custom-call | tf_op jit(solution)/shard_map/finish/pallas_call | solution.py:287
  (2 shorter events, 0.1 us)
Async XLA Ops:
  1.9 1.0 %copy-start = (bf16[1,8,16384]{2,1,0:T(8,128)(2,1)S(1)}, bf16[1,8,16384]{2,1,0:T(8,128)(2,1)}, u32[]{:S(2)}) copy-start(bf16[1,8,16384]{2,1,0:T(8,128)(2,1)} %param.5) | copy-start | bytes 786436
  2.9 0.7 copy-start.4
  4.3 13.0 %collective-permute-start = (bf16[8,2560]{1,0:T(8,128)(2,1)S(1)}, bf16[8,2560]{1,0:T(8,128)(2,1)S(1)}, u32[]{:S(2)}, u32[]{:S(2)}) collective-permute-start(bf16[8,2560]{1,0:T(8,128)(2,1)S(1)} %get-tuple-element.17), channel_id=1, source_target_pairs={{0,4},{4,8},{8,12},{12,16},{16,20},{20,24},{24,28},{28,32},{32,36}... | collective-permute-start | bytes 122888 | tf_op jit(solution)/shard_map/ppermute | solution.py:308
  8.8 8.5 %collective-permute-start.1 = (bf16[8,2560]{1,0:T(8,128)(2,1)S(1)}, bf16[8,2560]{1,0:T(8,128)(2,1)S(1)}, u32[]{:S(2)}, u32[]{:S(2)}) collective-permute-start(bf16[8,2560]{1,0:T(8,128)(2,1)S(1)} %get-tuple-element.18), channel_id=1, source_target_pairs={{4,0},{8,4},{12,8},{16,12},{20,16},{24,20},{28,24},{32,28},{36,32}... | collective-permute-start | bytes 122888 | tf_op jit(solution)/shard_map/ppermute | solution.py:309
  14.4 0.9 %copy-start.1 = (bf16[27,32,32]{2,1,0:T(8,128)(2,1)S(1)}, bf16[27,32,32]{2,1,0:T(8,128)(2,1)}, u32[]{:S(2)}) copy-start(bf16[27,32,32]{2,1,0:T(8,128)(2,1)} %conv.3) | copy-start | bytes 165892
  15.3 0.8 %copy-start.3 = (bf16[8,32,64]{2,1,0:T(8,128)(2,1)S(1)}, bf16[8,32,64]{2,1,0:T(8,128)(2,1)}, u32[]{:S(2)}) copy-start(bf16[8,32,64]{2,1,0:T(8,128)(2,1)} %down.1) | copy-start | bytes 98308
  23.4 49.5 %copy-start.2 = (bf16[27,32,32]{2,1,0:T(8,128)(2,1)S(1)}, bf16[27,32,32]{2,1,0:T(8,128)(2,1)}, u32[]{:S(2)}) copy-start(bf16[27,32,32]{2,1,0:T(8,128)(2,1)} %conv.3) | copy-start | bytes 165892
  23.5 49.5 %copy-start.5 = (s32[1,8]{1,0:T(1,128)S(1)}, s32[1,8]{1,0:T(1,128)}, u32[]{:S(2)}) copy-start(s32[1,8]{1,0:T(1,128)} %active.5) | copy-start | bytes 100
  65.7 16.2 %all-to-all-start.2 = ((f32[32,16,128]{2,1,0:T(8,128)}), f32[32,16,128]{2,1,0:T(8,128)S(1)}, u32[]{:S(2)}, u32[]{:S(2)}) async-start(f32[32,16,128]{2,1,0:T(8,128)} %sum_far.1), calls=%async_computation.2 | async-start | bytes 524288 | tf_op jit(solution)/shard_map/all_to_all | solution.py:338

commit v2 on v1

v2 whole, which is shorter than its diff:
```python
import jax
import jax.numpy as jnp
from jax import lax
from jax.experimental import pallas as pl
from jax.experimental.pallas import tpu as pltpu
from jax.sharding import Mesh
from jax.sharding import PartitionSpec as P

BLOCKS = ("z", "x", "core")
NEAR = ("x", "core", "vol")
F32 = jnp.float32
BF16 = jnp.bfloat16

ROW = 256
WIDE = 384
PIECE = 16


def iota(shape, dim):
    return lax.broadcasted_iota(jnp.int32, shape, dim)


def live_rows(active_ref):
    slot = iota((8, ROW), 0)
    out = jnp.zeros((8, ROW), F32)
    for b in range(8):
        out = jnp.where(slot == b, active_ref[0, b].astype(F32), out)
    return out


def repeat_lanes(rows, lanes):
    return (iota((rows, lanes), 1) % rows == iota((rows, lanes), 0)).astype(BF16)


def widen(row, halves):
    slot, lane = iota((8, 128), 0), iota((8, 128), 1)
    first, second = row[:, :128], row[:, 128:]
    right = pltpu.roll(first, 7, 0)
    left = pltpu.roll(second, 1, 0)
    edge = jnp.where(
        (slot % 2 == 0) & (lane < 32), right, jnp.where((slot % 2 == 1) & (lane >= 96), left, 0.0)
    )
    parts = [first, second, edge]
    if halves:
        parts += [jnp.where(lane >= 96, edge, second), jnp.where(lane < 32, edge, first)]
    return jnp.concatenate(parts, axis=1)


def put_plane(outer, inner, z, rows, halves=True):
    full = [widen(row, halves) for row in rows]
    upper = (iota(full[0].shape, 0) // 2) % 2
    low = jnp.where(upper == 1, pltpu.roll(full[7], 2, 0), 0.0)
    high = jnp.where(upper == 0, pltpu.roll(full[0], 6, 0), 0.0)
    ring = [low] + full + [high]
    for k in range(5):
        outer[z, 16 * k : 16 * k + 16] = jnp.concatenate(ring[2 * k : 2 * k + 2], 0).astype(BF16)
    for k in range(4):
        inner[z, 16 * k : 16 * k + 16] = jnp.concatenate(full[2 * k : 2 * k + 2], 0).astype(BF16)


def window(outer, inner, first, count, oz, oy, lanes):
    source = inner if oy == 1 else outer
    start = 16 if oy == 2 else 0
    rows = source[first + oz : first + oz + count, start : start + 64, lanes]
    return rows.reshape(count * 64, rows.shape[-1])


def convolve(outer, inner, bands, first, count):
    left = [
        window(outer, inner, first, count, index // 3, index % 3, slice(0, WIDE)) for index in range(9)
    ]
    return jnp.dot(
        jnp.concatenate(left, 1), bands[...].reshape(9 * WIDE, ROW), preferred_element_type=F32
    )


def slopes(pre, dy, fine):
    sig = 0.5 * jnp.tanh(0.5 * pre) + 0.5
    silu = pre * sig
    return (dy * sig * (1.0 + (pre - silu))).astype(BF16), fine + silu


def put_state(state, z, rows):
    for qy in range(2):
        for half in range(2):
            pair = [rows[2 * half + k][8 * qy : 8 * qy + 8] for k in range(2)]
            start = 32 * (z // 2) + 16 * half
            state[2 * (z % 2) + qy, start : start + 16] = jnp.concatenate(pair, 0).astype(BF16)


def put_bands(bands, index, taps):
    spot = iota((32, ROW), 1) // 32
    for i in range(8):
        part = jnp.zeros((32, ROW), F32)
        for ox in range(3):
            part = jnp.where(spot == i + 1 - ox, taps[ox], part)
        bands[index, 32 * i : 32 * i + 32] = part.astype(BF16)
    bands[index, 256:288] = jnp.where(spot == 7, taps[2], 0.0).astype(BF16)
    bands[index, 288:352] = jnp.zeros((64, ROW), BF16)
    bands[index, 352:384] = jnp.where(spot == 0, taps[0], 0.0).astype(BF16)


def pack_kernel(
    active, features, coarse, conv, down, to_next, to_prev, coarse_rows, live_out, fine_out, conv_out, down_out,
    flags, flat, sems,
):
    ends = [slice(0, 4096), slice(12288, 16384), slice(4096, 12288)]
    copies = [
        pltpu.make_async_copy(active, flags, sems.at[0]),
        pltpu.make_async_copy(coarse, flat, sems.at[1]),
    ]
    copies += [
        pltpu.make_async_copy(features.at[:, lanes], fine_out.at[:, lanes], sems.at[2 + k])
        for k, lanes in enumerate(ends)
    ]
    copies += [
        pltpu.make_async_copy(conv, conv_out, sems.at[5]),
        pltpu.make_async_copy(down, down_out, sems.at[6]),
    ]
    for copy in copies:
        copy.start()
    copies[0].wait()
    live = live_rows(flags)
    live_out[...] = live
    slot = iota((8, ROW), 0)
    copies[1].wait()

    def coarse_row(zc, yc):
        parts = []
        for b in range(8):
            start = ((((b // 4) * 4 + zc) * 8 + ((b // 2) % 2) * 4 + yc) * 2 + b % 2) * ROW
            parts.append(flat[:, start : start + ROW].astype(F32))
        return jnp.concatenate(parts, 0) * live

    ends = {}
    for zc in range(4):
        for half in range(2):
            both = [coarse_row(zc, 2 * half + k) for k in range(2)]
            start = 32 * zc + 16 * half
            coarse_rows[start : start + 16] = jnp.concatenate(both, 0).astype(BF16)
            ends[zc, half] = both
    for half in range(2):
        lanes = slice(2048 + half * ROW, 2048 + half * ROW + ROW)
        last, first = ends[3, half], ends[0, half]
        to_next[:, lanes] = jnp.where(slot < 4, pltpu.roll(last[0], 4, 0), last[1]).astype(BF16)
        to_prev[:, lanes] = jnp.where(slot < 4, first[1], pltpu.roll(first[0], 4, 0)).astype(BF16)

    def fine(z, y):
        start = (z * 8 + y) * ROW
        return fine_out[:, start : start + ROW].astype(F32) * live

    copies[2].wait()
    copies[3].wait()
    for y in range(8):
        lanes = slice(y * ROW, y * ROW + ROW)
        to_next[:, lanes] = jnp.where(slot < 4, pltpu.roll(fine(6, y), 4, 0), fine(7, y)).astype(BF16)
        to_prev[:, lanes] = jnp.where(slot < 4, fine(1, y), pltpu.roll(fine(0, y), 4, 0)).astype(BF16)
    for copy in copies[4:]:
        copy.wait()


def inner_kernel(
    live_in, features, conv, down, coarse, outer, inner, bands, spread, dpre, dy, state, pre, spread_out,
):
    live = live_in[...]
    tile = repeat_lanes(32, ROW)
    spot = iota((64, ROW), 1) // 32
    for q in range(4):
        turned = [
            lax.dot_general(down[2 * q + ox], tile, (((0,), (0,)), ((), ())), preferred_element_type=F32)
            for ox in range(2)
        ]
        for cx in range(4):
            part = jnp.where(spot == 2 * cx, turned[0], jnp.where(spot == 2 * cx + 1, turned[1], 0.0))
            spread[64 * cx : 64 * cx + 64, ROW * q : ROW * q + ROW] = part.astype(BF16)
    spread_out[...] = jnp.dot(coarse[...], spread[...], preferred_element_type=F32)
    taps = jnp.dot(conv[...].reshape(27 * 32, 32), tile, preferred_element_type=F32)
    for index in range(9):
        put_bands(bands, index, [taps[96 * index + 32 * ox : 96 * index + 32 * ox + 32] for ox in range(3)])
    for z in range(8):
        rows = []
        for y in range(8):
            start = (z * 8 + y) * ROW
            rows.append(features[:, start : start + ROW].astype(F32) * live)
        put_plane(outer, inner, z, rows)
    pre[...] = convolve(outer, inner, bands, 0, 6)
    for z in range(8):
        qz, rows = z % 2, []
        for pair in range(4):
            part = slice(16 * pair, 16 * pair + 16)
            base = 32 * (z // 2) + 8 * pair
            lanes = [slice(ROW * (2 * qz + qy), ROW * (2 * qz + qy) + ROW) for qy in range(2)]
            spread_rows = jnp.concatenate([spread_out[base : base + 8, lane] for lane in lanes], 0)
            dy[z, part] = spread_rows
            if 1 <= z <= 6:
                start = 64 * (z - 1) + 16 * pair
                fine = inner[z, part, :ROW].astype(F32)
                dpre[z - 1, part], y = slopes(pre[start : start + 16], spread_rows, fine)
                rows.append(y)
        if rows:
            put_state(state, z, rows)
    for z in (0, 7):
        put_state(state, z, [jnp.zeros((16, ROW), F32)] * 4)


def main_kernel(
    scale, inner_own, outer_own, from_prev, from_next, coarse, bands, spread, dpre_own, dy, state_own,
    grads, dpre, outer, inner, ends, pre, state,
):
    slot = iota((8, ROW), 0)
    outer[2:10] = outer_own[...]
    inner[2:10] = inner_own[...]
    dpre[2:8] = dpre_own[...]
    state[...] = state_own[...]

    def own(z, y):
        return inner_own[z, 16 * (y // 2) : 16 * (y // 2) + 16, :ROW].astype(F32)[8 * (y % 2) : 8 * (y % 2) + 8]

    before, beyond, after, past = [], [], [], []
    for y in range(8):
        low = from_prev[:, y * ROW : y * ROW + ROW].astype(F32)
        high = from_next[:, y * ROW : y * ROW + ROW].astype(F32)
        beyond.append(jnp.where(slot < 4, low, pltpu.roll(own(6, y), 4, 0)))
        before.append(pltpu.roll(jnp.where(slot >= 4, low, own(7, y)), 4, 0))
        after.append(jnp.where(slot >= 4, high, pltpu.roll(own(0, y), 4, 0)))
        past.append(pltpu.roll(jnp.where(slot < 4, high, own(1, y)), 4, 0))
    for z, rows in ((0, beyond), (1, before), (10, after), (11, past)):
        put_plane(outer, inner, z, rows)

    for k in range(2):
        lanes = slice(2048 + k * ROW, 2048 + k * ROW + ROW)
        low, high = from_prev[:, lanes].astype(F32), from_next[:, lanes].astype(F32)
        last = coarse[96 + 16 * k : 112 + 16 * k].astype(F32)
        first = coarse[16 * k : 16 * k + 16].astype(F32)
        under = [
            jnp.where(slot < 4, low, pltpu.roll(last[:8], 4, 0)),
            pltpu.roll(jnp.where(slot >= 4, low, last[8:]), 4, 0),
        ]
        over = [
            jnp.where(slot >= 4, high, pltpu.roll(first[:8], 4, 0)),
            pltpu.roll(jnp.where(slot < 4, high, first[8:]), 4, 0),
        ]
        ends[0, 16 * k : 16 * k + 16] = jnp.concatenate(under, 0).astype(BF16)
        ends[1, 16 * k : 16 * k + 16] = jnp.concatenate(over, 0).astype(BF16)
    dy_end = [
        jnp.dot(ends[0], spread[:, 2 * ROW :], preferred_element_type=F32),
        jnp.dot(ends[1], spread[:, : 2 * ROW], preferred_element_type=F32),
    ]

    for side in range(2):
        pre[side] = convolve(outer, inner, bands, 8 * side, 2)
    for side in range(2):
        for k in range(2):
            step = 8 * side + k
            z = step - 1
            rows = []
            for pair in range(4):
                part = slice(16 * pair, 16 * pair + 16)
                if 0 <= z < 8:
                    back = dy[z, part]
                else:
                    back = jnp.concatenate(
                        [dy_end[side][8 * pair : 8 * pair + 8, ROW * qy : ROW * qy + ROW] for qy in range(2)], 0
                    )
                start = 64 * k + 16 * pair
                fine = inner[step + 1, part, :ROW].astype(F32)
                dpre[step, part], y = slopes(pre[side, start : start + 16], back, fine)
                rows.append(y)
            if 0 <= z < 8:
                put_state(state, z, rows)

    lane = iota((32, 128), 1)
    v0, v1, low1, high1 = slice(0, 128), slice(128, 256), slice(384, 512), slice(512, 640)
    turned = dpre[1:9].reshape(512, ROW).T
    turned = jnp.concatenate([turned[:128], turned[128:]], 1)
    for oz in range(3):
        right = []
        for oy in range(3):
            halves = [
                jnp.concatenate([window(outer, inner, 1, 8, oz, oy, part) for part in parts], 1)
                for parts in ((v0, low1), (v1, high1))
            ]
            right.append(jnp.concatenate(halves, 0))
        products = jnp.dot(turned, jnp.concatenate(right, 1), preferred_element_type=F32)
        for oy in range(3):
            block = [products[32 * j : 32 * j + 32, ROW * oy : ROW * oy + ROW] for j in range(4)]
            t0 = jnp.where(lane >= 96, block[0][:, v1], block[0][:, v0])
            t3 = jnp.where(lane < 32, block[3][:, v1], block[3][:, v0])
            folded = (
                pltpu.roll(t0, 32, 1)
                + block[1][:, v0]
                + pltpu.roll(block[2][:, v0], 96, 1)
                + pltpu.roll(t3, 64, 1)
            )
            start = 32 * (3 * oz + oy)
            grads[start : start + 32] = jnp.where(lane < 96, folded * scale, 0.0)
    left = jnp.concatenate(
        [jnp.concatenate([state[q][:, v0], state[q][:, v1]], 0) for q in range(4)], 1
    )
    right = jnp.concatenate([coarse[:, v0], coarse[:, v1]], 0)
    products = lax.dot_general(left, right, (((0,), (0,)), ((), ())), preferred_element_type=F32)
    for q in range(4):
        block = [products[128 * q + 32 * x : 128 * q + 32 * x + 32] for x in range(4)]
        folded = jnp.where(lane < 64, block[0], block[3]) + pltpu.roll(
            jnp.where(lane < 64, block[1], block[2]), 64, 1
        )
        grads[288 + 32 * q : 320 + 32 * q] = folded * scale
    grads[416:512] = jnp.zeros((96, 128), F32)


def back_kernel(live_in, conv, dpre, dy, result, outer, inner, bands):
    live = live_in[...]
    tile = repeat_lanes(32, ROW)
    for index in range(9):
        taps = [
            lax.dot_general(
                conv[26 - (3 * index + ox)], tile, (((0,), (0,)), ((), ())), preferred_element_type=F32
            )
            for ox in range(3)
        ]
        put_bands(bands, index, taps)
    for z in range(10):
        rows = []
        for pair in range(4):
            both = dpre[z, 16 * pair : 16 * pair + 16].astype(F32)
            rows += [both[:8], both[8:]]
        put_plane(outer, inner, z, rows, halves=False)
    total = convolve(outer, inner, bands, 0, 8)
    for z in range(8):
        for y in range(8):
            row = 64 * z + 8 * y
            value = dy[z, 8 * y : 8 * y + 8] + live * total[row : row + 8]
            result[:, row * 32 : row * 32 + ROW] = value.astype(BF16)


def sum_kernel(parts, out):
    total = parts[0]
    for k in range(1, parts.shape[0]):
        total = total + parts[k]
    for k in range(out.shape[0]):
        out[k] = total.astype(out.dtype)


def finish_kernel(whole, conv_grad, down_grad):
    def rows(start, count):
        parts = []
        for piece in range(start // PIECE, (start + count) // PIECE):
            parts.append(whole[piece].astype(F32))
        return jnp.concatenate(parts, 0)

    for index in range(9):
        turned = rows(32 * index, 32).T
        for ox in range(3):
            conv_grad[3 * index + ox] = turned[32 * ox : 32 * ox + 32]
    for q in range(4):
        both = rows(288 + 32 * q, 32)
        down_grad[2 * q] = both[:, :64]
        down_grad[2 * q + 1] = pltpu.roll(both, 64, 1)[:, :64]


def call(kernel, outs, arrays, scratch=(), far=0, name=None):
    arrays = [pltpu.with_memory_space_constraint(a, pltpu.HBM) for a in arrays[:far]] + arrays[far:]
    spaces = [pltpu.HBM] * far + [pltpu.VMEM] * (len(arrays) - far)
    return pl.pallas_call(
        kernel,
        out_shape=[jax.ShapeDtypeStruct(shape, dtype) for shape, dtype in outs],
        in_specs=[pl.BlockSpec(memory_space=space) for space in spaces],
        out_specs=[pl.BlockSpec(memory_space=pltpu.VMEM)] * len(outs),
        scratch_shapes=scratch,
        compiler_params=pltpu.CompilerParams(vmem_limit_bytes=40 * 2**20),
        name=name,
    )(*arrays)


def shards(features, active, coarse_grad, conv_weight, down_weight):
    fine = features[0]
    devices = lax.axis_size(BLOCKS)
    scale = (lax.axis_size("vol") * devices * fine.size // 32) ** -0.5
    full = WIDE + ROW
    to_next, to_prev, coarse, live, fine, conv, down = call(
        pack_kernel,
        [
            ((8, 2560), BF16), ((8, 2560), BF16), ((128, ROW), BF16), ((8, ROW), F32),
            (fine.shape, BF16), (conv_weight.shape, BF16), (down_weight.shape, BF16),
        ],
        [active, fine, coarse_grad[0], conv_weight, down_weight],
        [
            pltpu.SMEM(active.shape, jnp.int32),
            pltpu.VMEM(coarse_grad.shape[1:], BF16),
            pltpu.SemaphoreType.DMA((7,)),
        ],
        far=5, name="pack",
    )
    up = [(i, i + 1) for i in range(devices - 1)]
    from_prev = lax.ppermute(to_next, BLOCKS, up)
    from_next = lax.ppermute(to_prev, BLOCKS, [(j, i) for i, j in up])
    outer, inner, bands, spread, dpre, dy, state = call(
        inner_kernel,
        [
            ((8, 80, full), BF16), ((8, 64, full), BF16), ((9, WIDE, ROW), BF16), ((ROW, 4 * ROW), BF16),
            ((6, 64, ROW), BF16), ((8, 64, ROW), F32), ((4, 128, ROW), BF16),
        ],
        [live, fine, conv, down, coarse],
        [pltpu.VMEM((384, ROW), F32), pltpu.VMEM((128, 4 * ROW), F32)],
        name="inner",
    )
    grads, dpre = call(
        lambda *refs: main_kernel(scale, *refs),
        [((512, 128), F32), ((10, 64, ROW), BF16)],
        [inner, outer, from_prev, from_next, coarse, bands, spread, dpre, dy, state],
        [
            pltpu.VMEM((12, 80, full), BF16), pltpu.VMEM((12, 64, full), BF16), pltpu.VMEM((2, 32, ROW), BF16),
            pltpu.VMEM((2, 128, ROW), F32), pltpu.VMEM((4, 128, ROW), BF16),
        ],
        name="main",
    )
    count, far = lax.axis_size(NEAR), lax.axis_size("z")
    pieces = 512 // PIECE
    cut = grads.reshape(count, pieces // count, PIECE, 128) if count != pieces else grads.reshape(count, PIECE, 128)
    cut = lax.all_to_all(cut, NEAR, 0, 0)
    (result,) = call(
        back_kernel, [((8, 64 * ROW), BF16)], [live, conv, dpre, dy],
        [
            pltpu.VMEM((10, 80, WIDE), BF16), pltpu.VMEM((10, 64, WIDE), BF16), pltpu.VMEM((9, WIDE, ROW), BF16),
        ],
        name="back",
    )
    (mine,) = call(sum_kernel, [((far,) + cut.shape[1:], F32)], [cut], name="sum_near")
    mine = lax.all_to_all(mine, "z", 0, 0)
    (mine,) = call(sum_kernel, [(cut.shape, BF16)], [mine], name="sum_far")
    whole = lax.all_to_all(mine, NEAR, 0, 0).reshape(pieces, PIECE, 128)
    conv_grad, down_grad = call(
        finish_kernel, [((27, 32, 32), F32), ((8, 32, 64), F32)], [whole], name="finish"
    )
    return result[None], conv_grad, down_grad


def solution(mesh):
    fine = Mesh(mesh.devices.reshape(-1, 4, 2, mesh.shape["vol"]), BLOCKS + ("vol",))
    placed = (P("vol", BLOCKS, None), P("vol", BLOCKS), P("vol", BLOCKS, None), P(), P())
    return jax.shard_map(
        shards,
        mesh=fine,
        in_specs=placed,
        out_specs=(P("vol", BLOCKS, None), P(), P()),
        check_vma=False,
    )
```

time: 83.3 us -> 74.9 us (0.90)
  Pallas kernels: 12.8 us -> 8.59 us
  local copies, waits for them, and re-layouts: 3.4 us -> 0 us
  other arithmetic: 1.26 us -> 0 us
  blocking collectives: 41.5 us -> 42.5 us
    pallas_call x7, Pallas kernels: 12.8 us -> 8.59 us  [call(): pl.pallas_call(kernel, out_shape=[jax.ShapeDtypeStruct(shape, dtype) for...]
    unnamed x12 -> x0, local copies, waits for them, and re-layouts: 3.38 us -> none
    unnamed x1 -> x0, other arithmetic: 1.26 us -> none
    all_to_all x1, blocking collectives: 14.9 us -> 16 us  [shards(): cut = lax.all_to_all(cut, NEAR, 0, 0)]
where the time goes in v2:
time: 74.9 us; the launch traced here: 74.6 us
  blocking collectives  42.5 us (57%)
  starting transfers between devices  17.3 us (23%)
  Pallas kernels  8.59 us (11%)
  waiting for transfers between devices  5.49 us (7%)
    all_to_all x1, blocking collectives, shards(): mine = lax.all_to_all(mine, 'z', 0, 0)  26.6 us
    all_to_all x1, blocking collectives, shards(): cut = lax.all_to_all(cut, NEAR, 0, 0)  16 us
    pallas_call x7, Pallas kernels, call(): pl.pallas_call(kernel, out_shape=[jax.ShapeDtypeStruct(shape, dtype) for...  8.59 us
    all_to_all x1, starting transfers between devices, shards(): whole = lax.all_to_all(mine, NEAR, 0, 0).reshape(pieces, PIECE, 128)  7.24 us
    ppermute x1, starting transfers between devices, shards(): from_next = lax.ppermute(to_prev, BLOCKS, [(j, i) for i, j in up])  5.57 us
    all_to_all x1, waiting for transfers between devices, shards(): whole = lax.all_to_all(mine, NEAR, 0, 0).reshape(pieces, PIECE, 128)  5.49 us
    ppermute x1, starting transfers between devices, shards(): from_prev = lax.ppermute(to_next, BLOCKS, up)  4.51 us
  transfers between devices with their start and end apart: 3, of which 1 were waited for; matrix products, arithmetic and copies ran while one was open for 0% of the time, Pallas kernels for 5%

profile of v2, /device:TPU:1, one launch (start us, length us, event | category | flops | bytes accessed | tf_op | source)
XLA Modules:
  0.0 74.6 jit_solution(2497652832155761737)
XLA Ops:
  0.6 1.2 %pack.1 = (bf16[8,2560]{1,0:T(8,128)(2,1)S(1)}, bf16[8,2560]{1,0:T(8,128)(2,1)S(1)}, bf16[128,256]{1,0:T(8,128)(2,1)S(1)}, f32[8,256]{1,0:T(8,128)S(1)}, bf16[8,...) custom-call(s32[1,8]{1,0:T(1,128)} %active.1, bf16[8,16384]{1,0:T(8,128)(2,1)} %bitcast.5, ...), custom_call_target="tpu_custom_call" | custom-call | tf_op jit(solution)/shard_map/pack/pallas_call | solution.py:364
  1.8 4.5 %collective-permute-start = (bf16[8,2560]{1,0:T(8,128)(2,1)S(1)}, bf16[8,2560]{1,0:T(8,128)(2,1)S(1)}, u32[]{:S(2)}, u32[]{:S(2)}) collective-permute-start(bf16[8,2560]{1,0:T(8,128)(2,1)S(1)} %get-tuple-element.28), channel_id=1, source_target_pairs={{0,4},{4,8},{8,12},{12,16},{16,20},{20,24},{24,28},{28,32},{32,36}... | collective-permute-start | bytes 122888 | tf_op jit(solution)/shard_map/ppermute | solution.py:395
  6.4 5.6 %collective-permute-start.1 = (bf16[8,2560]{1,0:T(8,128)(2,1)S(1)}, bf16[8,2560]{1,0:T(8,128)(2,1)S(1)}, u32[]{:S(2)}, u32[]{:S(2)}) collective-permute-start(bf16[8,2560]{1,0:T(8,128)(2,1)S(1)} %get-tuple-element.29), channel_id=1, source_target_pairs={{4,0},{8,4},{12,8},{16,12},{20,16},{24,20},{28,24},{32,28},{36,32}... | collective-permute-start | bytes 122888 | tf_op jit(solution)/shard_map/ppermute | solution.py:396
  11.9 1.8 %inner.1 = (bf16[8,80,640]{2,1,0:T(8,128)(2,1)S(1)}, bf16[8,64,640]{2,1,0:T(8,128)(2,1)S(1)}, bf16[9,384,256]{2,1,0:T(8,128)(2,1)S(1)}, bf16[256,1024]{1,0:T(8,1...) custom-call(f32[8,256]{1,0:T(8,128)S(1)} %get-tuple-element.21.live_in, ...), custom_call_target="tpu_custom_call" | custom-call | tf_op jit(solution)/shard_map/inner/pallas_call | solution.py:364
  13.7 0.0 collective-permute-done.refs_2_
  13.7 0.0 collective-permute-done.1.refs_3_
  13.7 1.8 %main.1 = (f32[512,128]{1,0:T(8,128)S(1)}, bf16[10,64,256]{2,1,0:T(8,128)(2,1)S(1)}) custom-call(bf16[8,64,640]{2,1,0:T(8,128)(2,1)S(1)} %get-tuple-element.26.refs_0_, bf16[8,80,640]{2,1,0:T(8,128)(2,1)S(1)} %get-tuple-element.27.refs_1_, bf16[8,2560]{1,0:T(8,128)(2,1)S(1)} %collective-permute-done.refs_2_, ...), custom_call_target="tpu_custom_call" | custom-call | tf_op jit(solution)/shard_map/main/pallas_call | solution.py:364
  15.5 16.0 %all_to_all.15.parts = f32[32,16,128]{2,1,0:T(8,128)S(1)} all-to-all(f32[32,16,128]{2,1,0:T(8,128)S(1)} %bitcast.4), channel_id=1, replica_groups=mesh['z'=16,'x'=4,'core'=2,'vol'=4] {'x','core','vol'}, dimensions={0} | all-to-all | bytes 524288 | tf_op jit(solution)/shard_map/all_to_all | solution.py:420
  31.5 26.6 %all_to_all.16.parts = f32[16,16,128]{2,1,0:T(8,128)S(1)} all-to-all(f32[16,16,128]{2,1,0:T(8,128)S(1)} %sum_near.1), channel_id=1, replica_groups=mesh['z'=16,'x'=4,'core'=2,'vol'=4] {'z'}, dimensions={0} | all-to-all | bytes 262144 | tf_op jit(solution)/shard_map/all_to_all | solution.py:429
  58.1 0.7 sum_far.1
  58.8 7.2 %all-to-all-start.2 = ((bf16[32,16,128]{2,1,0:T(8,128)(2,1)}), bf16[32,16,128]{2,1,0:T(8,128)(2,1)S(1)}, u32[]{:S(2)}, u32[]{:S(2)}) async-start(bf16[32,16,128]{2,1,0:T(8,128)(2,1)} %sum_far.1), calls=%async_computation.2 | async-start | bytes 262144 | tf_op jit(solution)/shard_map/all_to_all | solution.py:431
  66.0 2.2 %back.1 = bf16[8,16384]{1,0:T(8,128)(2,1)} custom-call(f32[8,256]{1,0:T(8,128)S(1)} %get-tuple-element.21.live_in, bf16[27,32,32]{2,1,0:T(8,128)(2,1)S(1)} %get-tuple-element.22.conv, bf16[10,64,256]{2,1,0:T(8,128)(2,1)S(1)} %get-tuple-element.35.dpre, f32[8,64,256]{2,1,0:T(8,128)S(1)} %get-tuple-element.33.refs_8_.dy), custom_call_target="tpu_custom_call" | custom-call | tf_op jit(solution)/shard_map/back/pallas_call | solution.py:364
  68.2 5.5 %all-to-all-done.2.whole = bf16[32,16,128]{2,1,0:T(8,128)(2,1)S(1)} async-done(((bf16[32,16,128]{2,1,0:T(8,128)(2,1)}), bf16[32,16,128]{2,1,0:T(8,128)(2,1)S(1)}, u32[]{:S(2)}, u32[]{:S(2)}) %all-to-all-start.2) | async-done | bytes 131104 | tf_op jit(solution)/shard_map/all_to_all | solution.py:431
  73.7 0.9 %finish.1 = (f32[27,32,32]{2,1,0:T(8,128)}, f32[8,32,64]{2,1,0:T(8,128)}) custom-call(bf16[32,16,128]{2,1,0:T(8,128)(2,1)S(1)} %all-to-all-done.2.whole), custom_call_target="tpu_custom_call" | custom-call | tf_op jit(solution)/shard_map/finish/pallas_call | solution.py:364
  (1 shorter events, 0.0 us)
Async XLA Ops:
  1.8 11.9 %collective-permute-start = (bf16[8,2560]{1,0:T(8,128)(2,1)S(1)}, bf16[8,2560]{1,0:T(8,128)(2,1)S(1)}, u32[]{:S(2)}, u32[]{:S(2)}) collective-permute-start(bf16[8,2560]{1,0:T(8,128)(2,1)S(1)} %get-tuple-element.28), channel_id=1, source_target_pairs={{0,4},{4,8},{8,12},{12,16},{16,20},{20,24},{24,28},{28,32},{32,36}... | collective-permute-start | bytes 122888 | tf_op jit(solution)/shard_map/ppermute | solution.py:395
  6.4 7.4 %collective-permute-start.1 = (bf16[8,2560]{1,0:T(8,128)(2,1)S(1)}, bf16[8,2560]{1,0:T(8,128)(2,1)S(1)}, u32[]{:S(2)}, u32[]{:S(2)}) collective-permute-start(bf16[8,2560]{1,0:T(8,128)(2,1)S(1)} %get-tuple-element.29), channel_id=1, source_target_pairs={{4,0},{8,4},{12,8},{16,12},{20,16},{24,20},{28,24},{32,28},{36,32}... | collective-permute-start | bytes 122888 | tf_op jit(solution)/shard_map/ppermute | solution.py:396
  58.8 14.9 %all-to-all-start.2 = ((bf16[32,16,128]{2,1,0:T(8,128)(2,1)}), bf16[32,16,128]{2,1,0:T(8,128)(2,1)S(1)}, u32[]{:S(2)}, u32[]{:S(2)}) async-start(bf16[32,16,128]{2,1,0:T(8,128)(2,1)} %sum_far.1), calls=%async_computation.2 | async-start | bytes 262144 | tf_op jit(solution)/shard_map/all_to_all | solution.py:431

commit v3 on v2

--- a/solution.py
+++ b/solution.py
@@ -1,3 +1,6 @@
+import functools
+import math
+
 import jax
 import jax.numpy as jnp
 from jax import lax
@@ -13,7 +16,8 @@
 
 ROW = 256
 WIDE = 384
-PIECE = 16
+GRADS = 384
+SENT = BF16
 
 
 def iota(shape, dim):
@@ -101,7 +105,7 @@
 
 
 def pack_kernel(
-    active, features, coarse, conv, down, to_next, to_prev, coarse_rows, live_out, fine_out, conv_out, down_out,
+    active, features, coarse, conv, down, to_core, to_chip, coarse_rows, live_out, fine_out, conv_out, down_out,
     flags, flat, sems,
 ):
     ends = [slice(0, 4096), slice(12288, 16384), slice(4096, 12288)]
@@ -139,11 +143,19 @@
             start = 32 * zc + 16 * half
             coarse_rows[start : start + 16] = jnp.concatenate(both, 0).astype(BF16)
             ends[zc, half] = both
+    second = lax.axis_index("core") == 1
+
+    def send(start, to_next, to_prev):
+        to_core[:, start : start + ROW] = jnp.where(second, to_prev, to_next).astype(BF16)
+        to_chip[:, start : start + ROW] = jnp.where(second, to_next, to_prev).astype(BF16)
+
     for half in range(2):
-        lanes = slice(2048 + half * ROW, 2048 + half * ROW + ROW)
         last, first = ends[3, half], ends[0, half]
-        to_next[:, lanes] = jnp.where(slot < 4, pltpu.roll(last[0], 4, 0), last[1]).astype(BF16)
-        to_prev[:, lanes] = jnp.where(slot < 4, first[1], pltpu.roll(first[0], 4, 0)).astype(BF16)
+        send(
+            2048 + half * ROW,
+            jnp.where(slot < 4, pltpu.roll(last[0], 4, 0), last[1]),
+            jnp.where(slot < 4, first[1], pltpu.roll(first[0], 4, 0)),
+        )
 
     def fine(z, y):
         start = (z * 8 + y) * ROW
@@ -152,9 +164,11 @@
     copies[2].wait()
     copies[3].wait()
     for y in range(8):
-        lanes = slice(y * ROW, y * ROW + ROW)
-        to_next[:, lanes] = jnp.where(slot < 4, pltpu.roll(fine(6, y), 4, 0), fine(7, y)).astype(BF16)
-        to_prev[:, lanes] = jnp.where(slot < 4, fine(1, y), pltpu.roll(fine(0, y), 4, 0)).astype(BF16)
+        send(
+            y * ROW,
+            jnp.where(slot < 4, pltpu.roll(fine(6, y), 4, 0), fine(7, y)),
+            jnp.where(slot < 4, fine(1, y), pltpu.roll(fine(0, y), 4, 0)),
+        )
     for copy in copies[4:]:
         copy.wait()
 
@@ -204,7 +218,7 @@
 
 
 def main_kernel(
-    scale, inner_own, outer_own, from_prev, from_next, coarse, bands, spread, dpre_own, dy, state_own,
+    scale, inner_own, outer_own, from_core, from_chip, coarse, bands, spread, dpre_own, dy, state_own,
     grads, dpre, outer, inner, ends, pre, state,
 ):
     slot = iota((8, ROW), 0)
@@ -213,13 +227,19 @@
     dpre[2:8] = dpre_own[...]
     state[...] = state_own[...]
 
+    second = lax.axis_index("core") == 1
+
+    def received(start):
+        core = from_core[:, start : start + ROW].astype(F32)
+        chip = from_chip[:, start : start + ROW].astype(F32)
+        return jnp.where(second, core, chip), jnp.where(second, chip, core)
+
     def own(z, y):
         return inner_own[z, 16 * (y // 2) : 16 * (y // 2) + 16, :ROW].astype(F32)[8 * (y % 2) : 8 * (y % 2) + 8]
 
     before, beyond, after, past = [], [], [], []
     for y in range(8):
-        low = from_prev[:, y * ROW : y * ROW + ROW].astype(F32)
-        high = from_next[:, y * ROW : y * ROW + ROW].astype(F32)
+        low, high = received(y * ROW)
         beyond.append(jnp.where(slot < 4, low, pltpu.roll(own(6, y), 4, 0)))
         before.append(pltpu.roll(jnp.where(slot >= 4, low, own(7, y)), 4, 0))
         after.append(jnp.where(slot >= 4, high, pltpu.roll(own(0, y), 4, 0)))
@@ -228,8 +248,7 @@
         put_plane(outer, inner, z, rows)
 
     for k in range(2):
-        lanes = slice(2048 + k * ROW, 2048 + k * ROW + ROW)
-        low, high = from_prev[:, lanes].astype(F32), from_next[:, lanes].astype(F32)
+        low, high = received(2048 + k * ROW)
         last = coarse[96 + 16 * k : 112 + 16 * k].astype(F32)
         first = coarse[16 * k : 16 * k + 16].astype(F32)
         under = [
@@ -273,6 +292,7 @@
     v0, v1, low1, high1 = slice(0, 128), slice(128, 256), slice(384, 512), slice(512, 640)
     turned = dpre[1:9].reshape(512, ROW).T
     turned = jnp.concatenate([turned[:128], turned[128:]], 1)
+    blocks = []
     for oz in range(3):
         right = []
         for oy in range(3):
@@ -292,8 +312,12 @@
                 + pltpu.roll(block[2][:, v0], 96, 1)
                 + pltpu.roll(t3, 64, 1)
             )
-            start = 32 * (3 * oz + oy)
-            grads[start : start + 32] = jnp.where(lane < 96, folded * scale, 0.0)
+            blocks.append(jnp.where(lane < 96, folded * scale, 0.0))
+    for index in range(8):
+        both = blocks[index]
+        if index < 3:
+            both = jnp.where(lane < 96, both, pltpu.roll(blocks[8], 96 - 32 * index, 1))
+        grads[32 * index : 32 * index + 32] = both.astype(SENT)
     left = jnp.concatenate(
         [jnp.concatenate([state[q][:, v0], state[q][:, v1]], 0) for q in range(4)], 1
     )
@@ -304,8 +328,7 @@
         folded = jnp.where(lane < 64, block[0], block[3]) + pltpu.roll(
             jnp.where(lane < 64, block[1], block[2]), 64, 1
         )
-        grads[288 + 32 * q : 320 + 32 * q] = folded * scale
-    grads[416:512] = jnp.zeros((96, 128), F32)
+        grads[256 + 32 * q : 288 + 32 * q] = (folded * scale).astype(SENT)
 
 
 def back_kernel(live_in, conv, dpre, dy, result, outer, inner, bands):
@@ -333,29 +356,34 @@
             result[:, row * 32 : row * 32 + ROW] = value.astype(BF16)
 
 
-def sum_kernel(parts, out):
-    total = parts[0]
-    for k in range(1, parts.shape[0]):
-        total = total + parts[k]
-    for k in range(out.shape[0]):
-        out[k] = total.astype(out.dtype)
+def sum_kernel(piece, parts, out):
+    unit = math.lcm(piece, 16)
+    total = parts[:unit].astype(F32)
+    for start in range(unit, parts.shape[0], unit):
+        total = total + parts[start : start + unit].astype(F32)
+    pieces = [total[start : start + piece] for start in range(0, unit, piece)]
+    total = sum(pieces[1:], pieces[0])
+    whole = jnp.concatenate([total] * len(pieces), 0).astype(out.dtype)
+    for start in range(0, out.shape[0], unit):
+        out[start : start + unit] = whole
 
 
 def finish_kernel(whole, conv_grad, down_grad):
-    def rows(start, count):
-        parts = []
-        for piece in range(start // PIECE, (start + count) // PIECE):
-            parts.append(whole[piece].astype(F32))
-        return jnp.concatenate(parts, 0)
-
-    for index in range(9):
-        turned = rows(32 * index, 32).T
+    for index in range(8):
+        turned = whole[32 * index : 32 * index + 32].astype(F32).T
         for ox in range(3):
             conv_grad[3 * index + ox] = turned[32 * ox : 32 * ox + 32]
+        if index < 3:
+            conv_grad[24 + index] = turned[96:]
     for q in range(4):
-        both = rows(288 + 32 * q, 32)
+        both = whole[256 + 32 * q : 288 + 32 * q].astype(F32)
         down_grad[2 * q] = both[:, :64]
         down_grad[2 * q + 1] = pltpu.roll(both, 64, 1)[:, :64]
+
+
+def exchange(rows, axes):
+    cut = rows.reshape(lax.axis_size(axes), -1, 4, 128)
+    return lax.all_to_all(cut, axes, 0, 0).reshape(rows.shape)
 
 
 def call(kernel, outs, arrays, scratch=(), far=0, name=None):
@@ -377,7 +405,7 @@
     devices = lax.axis_size(BLOCKS)
     scale = (lax.axis_size("vol") * devices * fine.size // 32) ** -0.5
     full = WIDE + ROW
-    to_next, to_prev, coarse, live, fine, conv, down = call(
+    to_core, to_chip, coarse, live, fine, conv, down = call(
         pack_kernel,
         [
             ((8, 2560), BF16), ((8, 2560), BF16), ((128, ROW), BF16), ((8, ROW), F32),
@@ -391,9 +419,9 @@
         ],
         far=5, name="pack",
     )
-    up = [(i, i + 1) for i in range(devices - 1)]
-    from_prev = lax.ppermute(to_next, BLOCKS, up)
-    from_next = lax.ppermute(to_prev, BLOCKS, [(j, i) for i, j in up])
+    pairs = [(i, i + 1) for i in range(1, devices - 1, 2)]
+    from_chip = lax.ppermute(to_chip, BLOCKS, pairs + [(j, i) for i, j in pairs])
+    from_core = lax.ppermute(to_core, "core", [(0, 1), (1, 0)])
     outer, inner, bands, spread, dpre, dy, state = call(
         inner_kernel,
         [
@@ -406,18 +434,17 @@
     )
     grads, dpre = call(
         lambda *refs: main_kernel(scale, *refs),
-        [((512, 128), F32), ((10, 64, ROW), BF16)],
-        [inner, outer, from_prev, from_next, coarse, bands, spread, dpre, dy, state],
+        [((GRADS, 128), SENT), ((10, 64, ROW), BF16)],
+        [inner, outer, from_core, from_chip, coarse, bands, spread, dpre, dy, state],
         [
             pltpu.VMEM((12, 80, full), BF16), pltpu.VMEM((12, 64, full), BF16), pltpu.VMEM((2, 32, ROW), BF16),
             pltpu.VMEM((2, 128, ROW), F32), pltpu.VMEM((4, 128, ROW), BF16),
         ],
         name="main",
     )
-    count, far = lax.axis_size(NEAR), lax.axis_size("z")
-    pieces = 512 // PIECE
-    cut = grads.reshape(count, pieces // count, PIECE, 128) if count != pieces else grads.reshape(count, PIECE, 128)
-    cut = lax.all_to_all(cut, NEAR, 0, 0)
+    near, far = lax.axis_size(NEAR), lax.axis_size("z")
+    add = functools.partial(sum_kernel, GRADS // near)
+    parts = exchange(grads, NEAR)
     (result,) = call(
         back_kernel, [((8, 64 * ROW), BF16)], [live, conv, dpre, dy],
         [
@@ -425,12 +452,10 @@
         ],
         name="back",
     )
-    (mine,) = call(sum_kernel, [((far,) + cut.shape[1:], F32)], [cut], name="sum_near")
-    mine = lax.all_to_all(mine, "z", 0, 0)
-    (mine,) = call(sum_kernel, [(cut.shape, BF16)], [mine], name="sum_far")
-    whole = lax.all_to_all(mine, NEAR, 0, 0).reshape(pieces, PIECE, 128)
+    (sums,) = call(add, [((far * GRADS // near, 128), SENT)], [parts], name="sum_near")
+    (sums,) = call(add, [((GRADS, 128), SENT)], [exchange(sums, "z")], name="sum_far")
     conv_grad, down_grad = call(
-        finish_kernel, [((27, 32, 32), F32), ((8, 32, 64), F32)], [whole], name="finish"
+        finish_kernel, [((27, 32, 32), F32), ((8, 32, 64), F32)], [exchange(sums, NEAR)], name="finish"
     )
     return result[None], conv_grad, down_grad
 

time: 74.9 us -> 69.6 us (0.929)
  blocking collectives: 42.5 us -> 37.1 us
  waiting for transfers between devices: 5.49 us -> 6.86 us
  starting transfers between devices: 17.3 us -> 16 us
    all_to_all x2, blocking collectives: 42.5 us -> 37.1 us  [exchange(): return lax.all_to_all(cut, axes, 0, 0).reshape(rows.shape)]
    all_to_all x1, starting transfers between devices: 7.24 us -> 5.34 us  [exchange(): return lax.all_to_all(cut, axes, 0, 0).reshape(rows.shape)]
    ppermute x2, waiting for transfers between devices: 0.01 us -> 1.62 us  [the longest x1 1.62 us: shards(): lax.ppermute(to_chip, BLOCKS, pairs + [(j, i) for i, j in pairs])]
  transfers between devices with their start and end apart: 3 -> 3, of which waited for: 1 -> 2; matrix products, arithmetic and copies ran while one was open for 0% -> 0% of each run, Pallas kernels for 5% -> 6%
where the time goes in v3:
time: 69.6 us; the launch traced here: 69.3 us
  blocking collectives  37.1 us (53%)
  starting transfers between devices  16 us (23%)
  Pallas kernels  8.64 us (12%)
  waiting for transfers between devices  6.86 us (10%)
    all_to_all x2, blocking collectives, exchange(): return lax.all_to_all(cut, axes, 0, 0).reshape(rows.shape)  37.1 us
    ppermute x1, starting transfers between devices, shards(): from_core = lax.ppermute(to_core, 'core', [(0, 1), (1, 0)])  8.79 us
    pallas_call x7, Pallas kernels, call(): pl.pallas_call(kernel, out_shape=[jax.ShapeDtypeStruct(shape, dtype) for...  8.64 us
    all_to_all x1, starting transfers between devices, exchange(): return lax.all_to_all(cut, axes, 0, 0).reshape(rows.shape)  5.34 us
    all_to_all x1, waiting for transfers between devices, exchange(): return lax.all_to_all(cut, axes, 0, 0).reshape(rows.shape)  5.24 us
    ppermute x1, starting transfers between devices, shards(): lax.ppermute(to_chip, BLOCKS, pairs + [(j, i) for i, j in pairs])  1.92 us
    ppermute x1, waiting for transfers between devices, shards(): lax.ppermute(to_chip, BLOCKS, pairs + [(j, i) for i, j in pairs])  1.62 us
  transfers between devices with their start and end apart: 3, of which 2 were waited for; matrix products, arithmetic and copies ran while one was open for 0% of the time, Pallas kernels for 6%

profile of v3, /device:TPU:1, one launch (start us, length us, event | category | flops | bytes accessed | tf_op | source)
XLA Modules:
  0.0 69.3 jit_solution(7085624929255948780)
XLA Ops:
  0.6 1.2 %pack.1 = (bf16[8,2560]{1,0:T(8,128)(2,1)S(1)}, bf16[8,2560]{1,0:T(8,128)(2,1)S(1)}, bf16[128,256]{1,0:T(8,128)(2,1)S(1)}, f32[8,256]{1,0:T(8,128)S(1)}, bf16[8,...) custom-call(s32[1,8]{1,0:T(1,128)} %active.1, bf16[8,16384]{1,0:T(8,128)(2,1)} %bitcast.14, ...), custom_call_target="tpu_custom_call" | custom-call | tf_op jit(solution)/shard_map/pack/pallas_call | solution.py:392
  1.8 8.8 %collective-permute-start = (bf16[8,2560]{1,0:T(8,128)(2,1)S(1)}, bf16[8,2560]{1,0:T(8,128)(2,1)S(1)}, u32[]{:S(2)}, u32[]{:S(2)}) collective-permute-start(bf16[8,2560]{1,0:T(8,128)(2,1)S(1)} %get-tuple-element.28), channel_id=1, source_target_pairs={{0,4},{4,0},{1,5},{5,1},{2,6},{6,2},{3,7},{7,3},{8,12},{12,8},{9,1... | collective-permute-start | bytes 122888 | tf_op jit(solution)/shard_map/ppermute | solution.py:424
  10.6 1.9 %collective-permute-start.1 = (bf16[8,2560]{1,0:T(8,128)(2,1)S(1)}, bf16[8,2560]{1,0:T(8,128)(2,1)S(1)}, u32[]{:S(2)}, u32[]{:S(2)}) collective-permute-start(bf16[8,2560]{1,0:T(8,128)(2,1)S(1)} %get-tuple-element.29), channel_id=1, source_target_pairs={{4,8},{12,16},{20,24},{28,32},{36,40},{44,48},{52,56},{60,64},{68,... | collective-permute-start | bytes 122888 | tf_op jit(solution)/shard_map/ppermute | solution.py:423
  12.6 1.8 %inner.1 = (bf16[8,80,640]{2,1,0:T(8,128)(2,1)S(1)}, bf16[8,64,640]{2,1,0:T(8,128)(2,1)S(1)}, bf16[9,384,256]{2,1,0:T(8,128)(2,1)S(1)}, bf16[256,1024]{1,0:T(8,1...) custom-call(f32[8,256]{1,0:T(8,128)S(1)} %get-tuple-element.21.live_in, ...), custom_call_target="tpu_custom_call" | custom-call | tf_op jit(solution)/shard_map/inner/pallas_call | solution.py:392
  14.3 0.0 collective-permute-done.refs_2_
  14.3 1.6 %collective-permute-done.1.refs_3_ = bf16[8,2560]{1,0:T(8,128)(2,1)S(1)} collective-permute-done((bf16[8,2560]{1,0:T(8,128)(2,1)S(1)}, bf16[8,2560]{1,0:T(8,128)(2,1)S(1)}, u32[]{:S(2)}, u32[]{:S(2)}) %collective-permute-start.1) | collective-permute-done | bytes 40992 | tf_op jit(solution)/shard_map/ppermute | solution.py:423
  16.0 1.9 %main.1 = (bf16[384,128]{1,0:T(8,128)(2,1)S(1)}, bf16[10,64,256]{2,1,0:T(8,128)(2,1)S(1)}) custom-call(bf16[8,64,640]{2,1,0:T(8,128)(2,1)S(1)} %get-tuple-element.26.refs_0_, bf16[8,80,640]{2,1,0:T(8,128)(2,1)S(1)} %get-tuple-element.27.refs_1_, bf16[8,2560]{1,0:T(8,128)(2,1)S(1)} %collective-permute-done.refs_2_, ...), custom_call_target="tpu_custom_call" | custom-call | tf_op jit(solution)/shard_map/main/pallas_call | solution.py:392
  17.8 10.8 %all_to_all.15 = bf16[32,3,4,128]{3,2,1,0:T(4,128)(2,1)S(1)} all-to-all(bf16[32,3,4,128]{3,2,1,0:T(4,128)(2,1)S(1)} %bitcast.13), channel_id=1, replica_groups=mesh['z'=16,'x'=4,'core'=2,'vol'=4] {'x','core','vol'}, dimensions={0} | all-to-all | bytes 196608 | tf_op jit(solution)/shard_map/all_to_all | solution.py:386
  28.7 26.3 %all_to_all.16 = bf16[16,3,4,128]{3,2,1,0:T(4,128)(2,1)S(1)} all-to-all(bf16[16,3,4,128]{3,2,1,0:T(4,128)(2,1)S(1)} %bitcast.11), channel_id=1, replica_groups=mesh['z'=16,'x'=4,'core'=2,'vol'=4] {'z'}, dimensions={0} | all-to-all | bytes 98304 | tf_op jit(solution)/shard_map/all_to_all | solution.py:386
  54.9 0.7 sum_far.1
  55.6 5.3 %all-to-all-start.2 = ((bf16[32,3,4,128]{3,2,1,0:T(4,128)(2,1)}), bf16[32,3,4,128]{3,2,1,0:T(4,128)(2,1)S(1)}, u32[]{:S(2)}, u32[]{:S(2)}) async-start(bf16[32,3,4,128]{3,2,1,0:T(4,128)(2,1)} %bitcast.7), calls=%async_computation.2 | async-start | bytes 196608 | tf_op jit(solution)/shard_map/all_to_all | solution.py:386
  60.9 2.2 %back.1 = bf16[8,16384]{1,0:T(8,128)(2,1)} custom-call(f32[8,256]{1,0:T(8,128)S(1)} %get-tuple-element.21.live_in, bf16[27,32,32]{2,1,0:T(8,128)(2,1)S(1)} %get-tuple-element.22.conv, bf16[10,64,256]{2,1,0:T(8,128)(2,1)S(1)} %get-tuple-element.35.dpre, f32[8,64,256]{2,1,0:T(8,128)S(1)} %get-tuple-element.33.refs_8_.dy), custom_call_target="tpu_custom_call" | custom-call | tf_op jit(solution)/shard_map/back/pallas_call | solution.py:392
  63.1 5.2 %all-to-all-done.2 = bf16[32,3,4,128]{3,2,1,0:T(4,128)(2,1)S(1)} async-done(((bf16[32,3,4,128]{3,2,1,0:T(4,128)(2,1)}), bf16[32,3,4,128]{3,2,1,0:T(4,128)(2,1)S(1)}, u32[]{:S(2)}, u32[]{:S(2)}) %all-to-all-start.2) | async-done | bytes 98336 | tf_op jit(solution)/shard_map/all_to_all | solution.py:386
  68.3 1.0 %finish.1 = (f32[27,32,32]{2,1,0:T(8,128)}, f32[8,32,64]{2,1,0:T(8,128)}) custom-call(bf16[384,128]{1,0:T(8,128)(2,1)S(1)} %bitcast.9), custom_call_target="tpu_custom_call" | custom-call | tf_op jit(solution)/shard_map/finish/pallas_call | solution.py:392
  (1 shorter events, 0.0 us)
Async XLA Ops:
  1.8 12.5 %collective-permute-start = (bf16[8,2560]{1,0:T(8,128)(2,1)S(1)}, bf16[8,2560]{1,0:T(8,128)(2,1)S(1)}, u32[]{:S(2)}, u32[]{:S(2)}) collective-permute-start(bf16[8,2560]{1,0:T(8,128)(2,1)S(1)} %get-tuple-element.28), channel_id=1, source_target_pairs={{0,4},{4,0},{1,5},{5,1},{2,6},{6,2},{3,7},{7,3},{8,12},{12,8},{9,1... | collective-permute-start | bytes 122888 | tf_op jit(solution)/shard_map/ppermute | solution.py:424
  10.6 5.3 %collective-permute-start.1 = (bf16[8,2560]{1,0:T(8,128)(2,1)S(1)}, bf16[8,2560]{1,0:T(8,128)(2,1)S(1)}, u32[]{:S(2)}, u32[]{:S(2)}) collective-permute-start(bf16[8,2560]{1,0:T(8,128)(2,1)S(1)} %get-tuple-element.29), channel_id=1, source_target_pairs={{4,8},{12,16},{20,24},{28,32},{36,40},{44,48},{52,56},{60,64},{68,... | collective-permute-start | bytes 122888 | tf_op jit(solution)/shard_map/ppermute | solution.py:423
  55.6 12.8 %all-to-all-start.2 = ((bf16[32,3,4,128]{3,2,1,0:T(4,128)(2,1)}), bf16[32,3,4,128]{3,2,1,0:T(4,128)(2,1)S(1)}, u32[]{:S(2)}, u32[]{:S(2)}) async-start(bf16[32,3,4,128]{3,2,1,0:T(4,128)(2,1)} %bitcast.7), calls=%async_computation.2 | async-start | bytes 196608 | tf_op jit(solution)/shard_map/all_to_all | solution.py:386

commit v4 on v3

--- a/solution.py
+++ b/solution.py
@@ -218,7 +218,7 @@
 
 
 def main_kernel(
-    scale, inner_own, outer_own, from_core, from_chip, coarse, bands, spread, dpre_own, dy, state_own,
+    scale, inner_own, outer_own, from_chip, from_core, coarse, bands, spread, dpre_own, dy, state_own,
     grads, dpre, outer, inner, ends, pre, state,
 ):
     slot = iota((8, ROW), 0)
@@ -435,7 +435,7 @@
     grads, dpre = call(
         lambda *refs: main_kernel(scale, *refs),
         [((GRADS, 128), SENT), ((10, 64, ROW), BF16)],
-        [inner, outer, from_core, from_chip, coarse, bands, spread, dpre, dy, state],
+        [inner, outer, from_chip, from_core, coarse, bands, spread, dpre, dy, state],
         [
             pltpu.VMEM((12, 80, full), BF16), pltpu.VMEM((12, 64, full), BF16), pltpu.VMEM((2, 32, ROW), BF16),
             pltpu.VMEM((2, 128, ROW), F32), pltpu.VMEM((4, 128, ROW), BF16),

time: 69.6 us -> 67.3 us (0.967)
  waiting for transfers between devices: 6.86 us -> 5.24 us
  starting transfers between devices: 16 us -> 14.8 us
    ppermute x1, starting transfers between devices: 8.79 us -> 4.94 us  [shards(): from_core = lax.ppermute(to_core, 'core', [(0, 1), (1, 0)])]
    ppermute x1, starting transfers between devices: 1.92 us -> 4.51 us  [shards(): lax.ppermute(to_chip, BLOCKS, pairs + [(j, i) for i, j in pairs])]
    ppermute x1, waiting for transfers between devices: 1.62 us -> 0.01 us  [shards(): lax.ppermute(to_chip, BLOCKS, pairs + [(j, i) for i, j in pairs])]
  transfers between devices with their start and end apart: 3 -> 3, of which waited for: 2 -> 1; matrix products, arithmetic and copies ran while one was open for 0% -> 0% of each run, Pallas kernels for 6% -> 6%
where the time goes in v4:
time: 67.3 us; the launch traced here: 67 us
  blocking collectives  37.7 us (56%)
  starting transfers between devices  14.8 us (22%)
  Pallas kernels  8.64 us (13%)
  waiting for transfers between devices  5.24 us (8%)
  between operations  0.7 us (1%)
    all_to_all x2, blocking collectives, exchange(): return lax.all_to_all(cut, axes, 0, 0).reshape(rows.shape)  37.7 us
    pallas_call x7, Pallas kernels, call(): pl.pallas_call(kernel, out_shape=[jax.ShapeDtypeStruct(shape, dtype) for...  8.64 us
    all_to_all x1, starting transfers between devices, exchange(): return lax.all_to_all(cut, axes, 0, 0).reshape(rows.shape)  5.34 us
    all_to_all x1, waiting for transfers between devices, exchange(): return lax.all_to_all(cut, axes, 0, 0).reshape(rows.shape)  5.24 us
    ppermute x1, starting transfers between devices, shards(): from_core = lax.ppermute(to_core, 'core', [(0, 1), (1, 0)])  4.94 us
    ppermute x1, starting transfers between devices, shards(): lax.ppermute(to_chip, BLOCKS, pairs + [(j, i) for i, j in pairs])  4.51 us
  transfers between devices with their start and end apart: 3, of which 1 were waited for; matrix products, arithmetic and copies ran while one was open for 0% of the time, Pallas kernels for 6%

profile of v4, /device:TPU:1, one launch (start us, length us, event | category | flops | bytes accessed | tf_op | source)
XLA Modules:
  0.0 67.0 jit_solution(6165600545526806413)
XLA Ops:
  0.6 1.2 %pack.1 = (bf16[8,2560]{1,0:T(8,128)(2,1)S(1)}, bf16[8,2560]{1,0:T(8,128)(2,1)S(1)}, bf16[128,256]{1,0:T(8,128)(2,1)S(1)}, f32[8,256]{1,0:T(8,128)S(1)}, bf16[8,...) custom-call(s32[1,8]{1,0:T(1,128)} %active.1, bf16[8,16384]{1,0:T(8,128)(2,1)} %bitcast.14, ...), custom_call_target="tpu_custom_call" | custom-call | tf_op jit(solution)/shard_map/pack/pallas_call | solution.py:392
  1.8 4.5 %collective-permute-start = (bf16[8,2560]{1,0:T(8,128)(2,1)S(1)}, bf16[8,2560]{1,0:T(8,128)(2,1)S(1)}, u32[]{:S(2)}, u32[]{:S(2)}) collective-permute-start(bf16[8,2560]{1,0:T(8,128)(2,1)S(1)} %get-tuple-element.28), channel_id=1, source_target_pairs={{4,8},{12,16},{20,24},{28,32},{36,40},{44,48},{52,56},{60,64},{68,... | collective-permute-start | bytes 122888 | tf_op jit(solution)/shard_map/ppermute | solution.py:423
  6.4 4.9 %collective-permute-start.1 = (bf16[8,2560]{1,0:T(8,128)(2,1)S(1)}, bf16[8,2560]{1,0:T(8,128)(2,1)S(1)}, u32[]{:S(2)}, u32[]{:S(2)}) collective-permute-start(bf16[8,2560]{1,0:T(8,128)(2,1)S(1)} %get-tuple-element.29), channel_id=1, source_target_pairs={{0,4},{4,0},{1,5},{5,1},{2,6},{6,2},{3,7},{7,3},{8,12},{12,8},{9,1... | collective-permute-start | bytes 122888 | tf_op jit(solution)/shard_map/ppermute | solution.py:424
  11.3 1.8 %inner.1 = (bf16[8,80,640]{2,1,0:T(8,128)(2,1)S(1)}, bf16[8,64,640]{2,1,0:T(8,128)(2,1)S(1)}, bf16[9,384,256]{2,1,0:T(8,128)(2,1)S(1)}, bf16[256,1024]{1,0:T(8,1...) custom-call(f32[8,256]{1,0:T(8,128)S(1)} %get-tuple-element.21.live_in, ...), custom_call_target="tpu_custom_call" | custom-call | tf_op jit(solution)/shard_map/inner/pallas_call | solution.py:392
  13.1 0.0 collective-permute-done.refs_2_
  13.1 0.0 collective-permute-done.1.refs_3_
  13.1 1.9 %main.1 = (bf16[384,128]{1,0:T(8,128)(2,1)S(1)}, bf16[10,64,256]{2,1,0:T(8,128)(2,1)S(1)}) custom-call(bf16[8,64,640]{2,1,0:T(8,128)(2,1)S(1)} %get-tuple-element.26.refs_0_, bf16[8,80,640]{2,1,0:T(8,128)(2,1)S(1)} %get-tuple-element.27.refs_1_, bf16[8,2560]{1,0:T(8,128)(2,1)S(1)} %collective-permute-done.refs_2_, ...), custom_call_target="tpu_custom_call" | custom-call | tf_op jit(solution)/shard_map/main/pallas_call | solution.py:392
  15.0 11.8 %all_to_all.15 = bf16[32,3,4,128]{3,2,1,0:T(4,128)(2,1)S(1)} all-to-all(bf16[32,3,4,128]{3,2,1,0:T(4,128)(2,1)S(1)} %bitcast.13), channel_id=1, replica_groups=mesh['z'=16,'x'=4,'core'=2,'vol'=4] {'x','core','vol'}, dimensions={0} | all-to-all | bytes 196608 | tf_op jit(solution)/shard_map/all_to_all | solution.py:386
  26.8 25.9 %all_to_all.16 = bf16[16,3,4,128]{3,2,1,0:T(4,128)(2,1)S(1)} all-to-all(bf16[16,3,4,128]{3,2,1,0:T(4,128)(2,1)S(1)} %bitcast.11), channel_id=1, replica_groups=mesh['z'=16,'x'=4,'core'=2,'vol'=4] {'z'}, dimensions={0} | all-to-all | bytes 98304 | tf_op jit(solution)/shard_map/all_to_all | solution.py:386
  52.7 0.7 sum_far.1
  53.3 5.3 %all-to-all-start.2 = ((bf16[32,3,4,128]{3,2,1,0:T(4,128)(2,1)}), bf16[32,3,4,128]{3,2,1,0:T(4,128)(2,1)S(1)}, u32[]{:S(2)}, u32[]{:S(2)}) async-start(bf16[32,3,4,128]{3,2,1,0:T(4,128)(2,1)} %bitcast.7), calls=%async_computation.2 | async-start | bytes 196608 | tf_op jit(solution)/shard_map/all_to_all | solution.py:386
  58.7 2.2 %back.1 = bf16[8,16384]{1,0:T(8,128)(2,1)} custom-call(f32[8,256]{1,0:T(8,128)S(1)} %get-tuple-element.21.live_in, bf16[27,32,32]{2,1,0:T(8,128)(2,1)S(1)} %get-tuple-element.22.conv, bf16[10,64,256]{2,1,0:T(8,128)(2,1)S(1)} %get-tuple-element.35.dpre, f32[8,64,256]{2,1,0:T(8,128)S(1)} %get-tuple-element.33.refs_8_.dy), custom_call_target="tpu_custom_call" | custom-call | tf_op jit(solution)/shard_map/back/pallas_call | solution.py:392
  60.8 5.2 %all-to-all-done.2 = bf16[32,3,4,128]{3,2,1,0:T(4,128)(2,1)S(1)} async-done(((bf16[32,3,4,128]{3,2,1,0:T(4,128)(2,1)}), bf16[32,3,4,128]{3,2,1,0:T(4,128)(2,1)S(1)}, u32[]{:S(2)}, u32[]{:S(2)}) %all-to-all-start.2) | async-done | bytes 98336 | tf_op jit(solution)/shard_map/all_to_all | solution.py:386
  66.1 1.0 %finish.1 = (f32[27,32,32]{2,1,0:T(8,128)}, f32[8,32,64]{2,1,0:T(8,128)}) custom-call(bf16[384,128]{1,0:T(8,128)(2,1)S(1)} %bitcast.9), custom_call_target="tpu_custom_call" | custom-call | tf_op jit(solution)/shard_map/finish/pallas_call | solution.py:392
  (1 shorter events, 0.0 us)
Async XLA Ops:
  1.8 11.2 %collective-permute-start = (bf16[8,2560]{1,0:T(8,128)(2,1)S(1)}, bf16[8,2560]{1,0:T(8,128)(2,1)S(1)}, u32[]{:S(2)}, u32[]{:S(2)}) collective-permute-start(bf16[8,2560]{1,0:T(8,128)(2,1)S(1)} %get-tuple-element.28), channel_id=1, source_target_pairs={{4,8},{12,16},{20,24},{28,32},{36,40},{44,48},{52,56},{60,64},{68,... | collective-permute-start | bytes 122888 | tf_op jit(solution)/shard_map/ppermute | solution.py:423
  6.4 6.7 %collective-permute-start.1 = (bf16[8,2560]{1,0:T(8,128)(2,1)S(1)}, bf16[8,2560]{1,0:T(8,128)(2,1)S(1)}, u32[]{:S(2)}, u32[]{:S(2)}) collective-permute-start(bf16[8,2560]{1,0:T(8,128)(2,1)S(1)} %get-tuple-element.29), channel_id=1, source_target_pairs={{0,4},{4,0},{1,5},{5,1},{2,6},{6,2},{3,7},{7,3},{8,12},{12,8},{9,1... | collective-permute-start | bytes 122888 | tf_op jit(solution)/shard_map/ppermute | solution.py:424
  53.3 12.8 %all-to-all-start.2 = ((bf16[32,3,4,128]{3,2,1,0:T(4,128)(2,1)}), bf16[32,3,4,128]{3,2,1,0:T(4,128)(2,1)S(1)}, u32[]{:S(2)}, u32[]{:S(2)}) async-start(bf16[32,3,4,128]{3,2,1,0:T(4,128)(2,1)} %bitcast.7), calls=%async_computation.2 | async-start | bytes 196608 | tf_op jit(solution)/shard_map/all_to_all | solution.py:386

commit v5 on v4

--- a/solution.py
+++ b/solution.py
@@ -381,9 +381,9 @@
         down_grad[2 * q + 1] = pltpu.roll(both, 64, 1)[:, :64]
 
 
-def exchange(rows, axes):
+def exchange(rows, axes, groups=None):
     cut = rows.reshape(lax.axis_size(axes), -1, 4, 128)
-    return lax.all_to_all(cut, axes, 0, 0).reshape(rows.shape)
+    return lax.all_to_all(cut, axes, 0, 0, axis_index_groups=groups).reshape(rows.shape)
 
 
 def call(kernel, outs, arrays, scratch=(), far=0, name=None):
@@ -398,6 +398,17 @@
         compiler_params=pltpu.CompilerParams(vmem_limit_bytes=40 * 2**20),
         name=name,
     )(*arrays)
+
+
+def opposite():
+    sizes = [lax.axis_size(axis) for axis in NEAR]
+    order = []
+    for x in range(sizes[0]):
+        for core in range(sizes[1]):
+            for vol in range(sizes[2]):
+                spot = (x + sizes[0] // 2) % sizes[0] * sizes[1] + (core + 1) % sizes[1]
+                order.append(spot * sizes[2] + (vol + sizes[2] // 2) % sizes[2])
+    return [order]
 
 
 def shards(features, active, coarse_grad, conv_weight, down_weight):
@@ -443,8 +454,9 @@
         name="main",
     )
     near, far = lax.axis_size(NEAR), lax.axis_size("z")
+    plane = opposite()
     add = functools.partial(sum_kernel, GRADS // near)
-    parts = exchange(grads, NEAR)
+    parts = exchange(grads, NEAR, plane)
     (result,) = call(
         back_kernel, [((8, 64 * ROW), BF16)], [live, conv, dpre, dy],
         [
@@ -453,9 +465,9 @@
         name="back",
     )
     (sums,) = call(add, [((far * GRADS // near, 128), SENT)], [parts], name="sum_near")
-    (sums,) = call(add, [((GRADS, 128), SENT)], [exchange(sums, "z")], name="sum_far")
+    (sums,) = call(add, [((GRADS, 128), SENT)], [exchange(sums, "z", [[(k + far // 2) % far for k in range(far)]])], name="sum_far")
     conv_grad, down_grad = call(
-        finish_kernel, [((27, 32, 32), F32), ((8, 32, 64), F32)], [exchange(sums, NEAR)], name="finish"
+        finish_kernel, [((27, 32, 32), F32), ((8, 32, 64), F32)], [exchange(sums, NEAR, plane)], name="finish"
     )
     return result[None], conv_grad, down_grad
 

time: 67.3 us -> 58.3 us (0.87)
  blocking collectives: 37.7 us -> 29.6 us
  waiting for transfers between devices: 5.24 us -> 0.44 us
  starting transfers between devices: 14.8 us -> 18.7 us
    all_to_all x2, blocking collectives: 37.7 us -> 29.6 us  [exchange(): lax.all_to_all(cut, axes, 0, 0, axis_index_groups=groups)]
    all_to_all x1, waiting for transfers between devices: 5.24 us -> 0.44 us  [exchange(): lax.all_to_all(cut, axes, 0, 0, axis_index_groups=groups)]
    all_to_all x1, starting transfers between devices: 5.34 us -> 9.25 us  [exchange(): lax.all_to_all(cut, axes, 0, 0, axis_index_groups=groups)]
  transfers between devices with their start and end apart: 3 -> 3, of which waited for: 1 -> 1; matrix products, arithmetic and copies ran while one was open for 0% -> 0% of each run, Pallas kernels for 6% -> 7%
where the time goes in v5:
time: 58.3 us; the launch traced here: 58.1 us
  blocking collectives  29.6 us (51%)
  starting transfers between devices  18.7 us (32%)
  Pallas kernels  8.64 us (15%)
  between operations  0.7 us (1%)
    all_to_all x2, blocking collectives, exchange(): lax.all_to_all(cut, axes, 0, 0, axis_index_groups=groups)  29.6 us
    all_to_all x1, starting transfers between devices, exchange(): lax.all_to_all(cut, axes, 0, 0, axis_index_groups=groups)  9.25 us
    pallas_call x7, Pallas kernels, call(): pl.pallas_call(kernel, out_shape=[jax.ShapeDtypeStruct(shape, dtype) for...  8.64 us
    ppermute x1, starting transfers between devices, shards(): from_core = lax.ppermute(to_core, 'core', [(0, 1), (1, 0)])  4.94 us
    ppermute x1, starting transfers between devices, shards(): lax.ppermute(to_chip, BLOCKS, pairs + [(j, i) for i, j in pairs])  4.51 us
  transfers between devices with their start and end apart: 3, of which 1 were waited for; matrix products, arithmetic and copies ran while one was open for 0% of the time, Pallas kernels for 7%

profile of v5, /device:TPU:1, one launch (start us, length us, event | category | flops | bytes accessed | tf_op | source)
XLA Modules:
  0.0 58.1 jit_solution(17983937682496802655)
XLA Ops:
  0.6 1.2 %pack.1 = (bf16[8,2560]{1,0:T(8,128)(2,1)S(1)}, bf16[8,2560]{1,0:T(8,128)(2,1)S(1)}, bf16[128,256]{1,0:T(8,128)(2,1)S(1)}, f32[8,256]{1,0:T(8,128)S(1)}, bf16[8,...) custom-call(s32[1,8]{1,0:T(1,128)} %active.1, bf16[8,16384]{1,0:T(8,128)(2,1)} %bitcast.14, ...), custom_call_target="tpu_custom_call" | custom-call | tf_op jit(solution)/shard_map/pack/pallas_call | solution.py:392
  1.8 4.5 %collective-permute-start = (bf16[8,2560]{1,0:T(8,128)(2,1)S(1)}, bf16[8,2560]{1,0:T(8,128)(2,1)S(1)}, u32[]{:S(2)}, u32[]{:S(2)}) collective-permute-start(bf16[8,2560]{1,0:T(8,128)(2,1)S(1)} %get-tuple-element.28), channel_id=1, source_target_pairs={{4,8},{12,16},{20,24},{28,32},{36,40},{44,48},{52,56},{60,64},{68,... | collective-permute-start | bytes 122888 | tf_op jit(solution)/shard_map/ppermute | solution.py:434
  6.4 4.9 %collective-permute-start.1 = (bf16[8,2560]{1,0:T(8,128)(2,1)S(1)}, bf16[8,2560]{1,0:T(8,128)(2,1)S(1)}, u32[]{:S(2)}, u32[]{:S(2)}) collective-permute-start(bf16[8,2560]{1,0:T(8,128)(2,1)S(1)} %get-tuple-element.29), channel_id=1, source_target_pairs={{0,4},{4,0},{1,5},{5,1},{2,6},{6,2},{3,7},{7,3},{8,12},{12,8},{9,1... | collective-permute-start | bytes 122888 | tf_op jit(solution)/shard_map/ppermute | solution.py:435
  11.3 1.8 %inner.1 = (bf16[8,80,640]{2,1,0:T(8,128)(2,1)S(1)}, bf16[8,64,640]{2,1,0:T(8,128)(2,1)S(1)}, bf16[9,384,256]{2,1,0:T(8,128)(2,1)S(1)}, bf16[256,1024]{1,0:T(8,1...) custom-call(f32[8,256]{1,0:T(8,128)S(1)} %get-tuple-element.21.live_in, ...), custom_call_target="tpu_custom_call" | custom-call | tf_op jit(solution)/shard_map/inner/pallas_call | solution.py:392
  13.1 0.0 collective-permute-done.refs_2_
  13.1 0.0 collective-permute-done.1.refs_3_
  13.1 1.9 %main.1 = (bf16[384,128]{1,0:T(8,128)(2,1)S(1)}, bf16[10,64,256]{2,1,0:T(8,128)(2,1)S(1)}) custom-call(bf16[8,64,640]{2,1,0:T(8,128)(2,1)S(1)} %get-tuple-element.26.refs_0_, bf16[8,80,640]{2,1,0:T(8,128)(2,1)S(1)} %get-tuple-element.27.refs_1_, bf16[8,2560]{1,0:T(8,128)(2,1)S(1)} %collective-permute-done.refs_2_, ...), custom_call_target="tpu_custom_call" | custom-call | tf_op jit(solution)/shard_map/main/pallas_call | solution.py:392
  15.0 9.2 %all_to_all.15 = bf16[32,3,4,128]{3,2,1,0:T(4,128)(2,1)S(1)} all-to-all(bf16[32,3,4,128]{3,2,1,0:T(4,128)(2,1)S(1)} %bitcast.13), channel_id=1, replica_groups={{22,23,20,21,18,19,16,17,30,31,28,29,26,27,24,25,6,7,4,5,2,3,0,1,14,15,..., dimensions={0} | all-to-all | bytes 196608 | tf_op jit(solution)/shard_map/all_to_all | solution.py:386
  24.2 20.3 %all_to_all.16 = bf16[16,3,4,128]{3,2,1,0:T(4,128)(2,1)S(1)} all-to-all(bf16[16,3,4,128]{3,2,1,0:T(4,128)(2,1)S(1)} %bitcast.11), channel_id=1, replica_groups={{256,288,320,352,384,416,448,480,0,32,64,96,128,160,192,224},{257,289,3..., dimensions={0} | all-to-all | bytes 98304 | tf_op jit(solution)/shard_map/all_to_all | solution.py:386
  44.6 0.7 %sum_far.1 = bf16[384,128]{1,0:T(8,128)(2,1)} custom-call(bf16[192,128]{1,0:T(8,128)(2,1)S(1)} %bitcast.12), custom_call_target="tpu_custom_call" | custom-call | tf_op jit(solution)/shard_map/sum_far/pallas_call | solution.py:392
  45.2 9.3 %all-to-all-start.2 = ((bf16[32,3,4,128]{3,2,1,0:T(4,128)(2,1)}), bf16[32,3,4,128]{3,2,1,0:T(4,128)(2,1)S(1)}, u32[]{:S(2)}, u32[]{:S(2)}) async-start(bf16[32,3,4,128]{3,2,1,0:T(4,128)(2,1)} %bitcast.7), calls=%async_computation.2 | async-start | bytes 196608 | tf_op jit(solution)/shard_map/all_to_all | solution.py:386
  54.5 2.2 %back.1 = bf16[8,16384]{1,0:T(8,128)(2,1)} custom-call(f32[8,256]{1,0:T(8,128)S(1)} %get-tuple-element.21.live_in, bf16[27,32,32]{2,1,0:T(8,128)(2,1)S(1)} %get-tuple-element.22.conv, bf16[10,64,256]{2,1,0:T(8,128)(2,1)S(1)} %get-tuple-element.35.dpre, f32[8,64,256]{2,1,0:T(8,128)S(1)} %get-tuple-element.33.refs_8_.dy), custom_call_target="tpu_custom_call" | custom-call | tf_op jit(solution)/shard_map/back/pallas_call | solution.py:392
  56.7 0.4 all-to-all-done.2
  57.1 1.0 %finish.1 = (f32[27,32,32]{2,1,0:T(8,128)}, f32[8,32,64]{2,1,0:T(8,128)}) custom-call(bf16[384,128]{1,0:T(8,128)(2,1)S(1)} %bitcast.9), custom_call_target="tpu_custom_call" | custom-call | tf_op jit(solution)/shard_map/finish/pallas_call | solution.py:392
  (1 shorter events, 0.0 us)
Async XLA Ops:
  1.8 11.2 %collective-permute-start = (bf16[8,2560]{1,0:T(8,128)(2,1)S(1)}, bf16[8,2560]{1,0:T(8,128)(2,1)S(1)}, u32[]{:S(2)}, u32[]{:S(2)}) collective-permute-start(bf16[8,2560]{1,0:T(8,128)(2,1)S(1)} %get-tuple-element.28), channel_id=1, source_target_pairs={{4,8},{12,16},{20,24},{28,32},{36,40},{44,48},{52,56},{60,64},{68,... | collective-permute-start | bytes 122888 | tf_op jit(solution)/shard_map/ppermute | solution.py:434
  6.4 6.7 %collective-permute-start.1 = (bf16[8,2560]{1,0:T(8,128)(2,1)S(1)}, bf16[8,2560]{1,0:T(8,128)(2,1)S(1)}, u32[]{:S(2)}, u32[]{:S(2)}) collective-permute-start(bf16[8,2560]{1,0:T(8,128)(2,1)S(1)} %get-tuple-element.29), channel_id=1, source_target_pairs={{0,4},{4,0},{1,5},{5,1},{2,6},{6,2},{3,7},{7,3},{8,12},{12,8},{9,1... | collective-permute-start | bytes 122888 | tf_op jit(solution)/shard_map/ppermute | solution.py:435
  45.2 11.9 %all-to-all-start.2 = ((bf16[32,3,4,128]{3,2,1,0:T(4,128)(2,1)}), bf16[32,3,4,128]{3,2,1,0:T(4,128)(2,1)S(1)}, u32[]{:S(2)}, u32[]{:S(2)}) async-start(bf16[32,3,4,128]{3,2,1,0:T(4,128)(2,1)} %bitcast.7), calls=%async_computation.2 | async-start | bytes 196608 | tf_op jit(solution)/shard_map/all_to_all | solution.py:386

commit v6 on v4

--- a/solution.py
+++ b/solution.py
@@ -1,4 +1,5 @@
 import functools
+import itertools
 import math
 
 import jax
@@ -197,7 +198,8 @@
             start = (z * 8 + y) * ROW
             rows.append(features[:, start : start + ROW].astype(F32) * live)
         put_plane(outer, inner, z, rows)
-    pre[...] = convolve(outer, inner, bands, 0, 6)
+    for z in range(0, 6, 2):
+        pre[64 * z : 64 * z + 128] = convolve(outer, inner, bands, z, 2)
     for z in range(8):
         qz, rows = z % 2, []
         for pair in range(4):
@@ -356,6 +358,18 @@
             result[:, row * 32 : row * 32 + ROW] = value.astype(BF16)
 
 
+def back_turn(turn, *refs):
+    *arrays, out, result, outer, inner, bands, sem = refs
+    first = lax.axis_index("z") * 8 < 3 * lax.axis_size("z")
+
+    @pl.when(first if turn == 0 else jnp.logical_not(first))
+    def _():
+        back_kernel(*arrays[turn:], result, outer, inner, bands)
+        copy = pltpu.make_async_copy(result, out, sem.at[0])
+        copy.start()
+        copy.wait()
+
+
 def sum_kernel(piece, parts, out):
     unit = math.lcm(piece, 16)
     total = parts[:unit].astype(F32)
@@ -381,23 +395,35 @@
         down_grad[2 * q + 1] = pltpu.roll(both, 64, 1)[:, :64]
 
 
-def exchange(rows, axes):
+def exchange(rows, axes, groups=None):
     cut = rows.reshape(lax.axis_size(axes), -1, 4, 128)
-    return lax.all_to_all(cut, axes, 0, 0).reshape(rows.shape)
-
-
-def call(kernel, outs, arrays, scratch=(), far=0, name=None):
+    return lax.all_to_all(cut, axes, 0, 0, axis_index_groups=groups).reshape(rows.shape)
+
+
+def call(kernel, outs, arrays, scratch=(), far=0, out_space=pltpu.VMEM, same=(), name=None):
     arrays = [pltpu.with_memory_space_constraint(a, pltpu.HBM) for a in arrays[:far]] + arrays[far:]
     spaces = [pltpu.HBM] * far + [pltpu.VMEM] * (len(arrays) - far)
     return pl.pallas_call(
         kernel,
         out_shape=[jax.ShapeDtypeStruct(shape, dtype) for shape, dtype in outs],
         in_specs=[pl.BlockSpec(memory_space=space) for space in spaces],
-        out_specs=[pl.BlockSpec(memory_space=pltpu.VMEM)] * len(outs),
+        out_specs=[pl.BlockSpec(memory_space=out_space)] * len(outs),
+        input_output_aliases=dict(same),
         scratch_shapes=scratch,
         compiler_params=pltpu.CompilerParams(vmem_limit_bytes=40 * 2**20),
         name=name,
     )(*arrays)
+
+
+def plane_order():
+    sizes = [lax.axis_size(axis) for axis in NEAR]
+    shift = [sizes[0] // 2, 1, sizes[2] // 2]
+    spots = itertools.product(*[range(size) for size in sizes])
+    return [
+        ((x + shift[0]) % sizes[0] * sizes[1] + (core + shift[1]) % sizes[1]) * sizes[2]
+        + (vol + shift[2]) % sizes[2]
+        for x, core, vol in spots
+    ]
 
 
 def shards(features, active, coarse_grad, conv_weight, down_weight):
@@ -443,20 +469,32 @@
         name="main",
     )
     near, far = lax.axis_size(NEAR), lax.axis_size("z")
+    plane = plane_order()
     add = functools.partial(sum_kernel, GRADS // near)
-    parts = exchange(grads, NEAR)
-    (result,) = call(
-        back_kernel, [((8, 64 * ROW), BF16)], [live, conv, dpre, dy],
-        [
-            pltpu.VMEM((10, 80, WIDE), BF16), pltpu.VMEM((10, 64, WIDE), BF16), pltpu.VMEM((9, WIDE, ROW), BF16),
-        ],
-        name="back",
-    )
+    parts = exchange(grads, NEAR, [plane])
+    def back(turn, arrays):
+        (result,) = call(
+            functools.partial(back_turn, turn), [((8, 64 * ROW), BF16)], arrays + [live, conv, dpre, dy],
+            [
+                pltpu.VMEM((8, 64 * ROW), BF16), pltpu.VMEM((10, 80, WIDE), BF16),
+                pltpu.VMEM((10, 64, WIDE), BF16), pltpu.VMEM((9, WIDE, ROW), BF16),
+                pltpu.SemaphoreType.DMA((1,)),
+            ],
+            far=turn, out_space=pltpu.HBM, same=[(0, 0)] * turn, name=f"back{turn}",
+        )
+        return result
+
+    parts, dpre = lax.optimization_barrier((parts, dpre))
+    result = back(0, [])
     (sums,) = call(add, [((far * GRADS // near, 128), SENT)], [parts], name="sum_near")
-    (sums,) = call(add, [((GRADS, 128), SENT)], [exchange(sums, "z")], name="sum_far")
+    sums, result = lax.optimization_barrier((sums, result))
+    sums = exchange(sums, "z", [[(k + far // 2) % far for k in range(far)]])
+    (sums,) = call(add, [((GRADS, 128), SENT)], [sums], name="sum_far")
+    whole, result = lax.optimization_barrier((exchange(sums, NEAR, [plane]), result))
     conv_grad, down_grad = call(
-        finish_kernel, [((27, 32, 32), F32), ((8, 32, 64), F32)], [exchange(sums, NEAR)], name="finish"
-    )
+        finish_kernel, [((27, 32, 32), F32), ((8, 32, 64), F32)], [whole], name="finish"
+    )
+    result = back(1, [result])
     return result[None], conv_grad, down_grad
 
 

time: 67.3 us -> 57.6 us (0.86)
  starting transfers between devices: 14.8 us -> 9.45 us
  waiting for transfers between devices: 5.24 us -> 0.01 us
  blocking collectives: 37.7 us -> 39.1 us
    all_to_all x1 -> x0, starting transfers between devices: 5.34 us -> none  [exchange(): return lax.all_to_all(cut, axes, 0, 0).reshape(rows.shape)]
    all_to_all x1 -> x0, waiting for transfers between devices: 5.24 us -> none  [exchange(): return lax.all_to_all(cut, axes, 0, 0).reshape(rows.shape)]
    all_to_all x2 -> x3, blocking collectives: 37.7 us -> 39.1 us  [exchange(): lax.all_to_all(cut, axes, 0, 0, axis_index_groups=groups)]
    pallas_call x7 -> x8, Pallas kernels: 8.64 us -> 8.14 us  [call(): pl.pallas_call(kernel, out_shape=[jax.ShapeDtypeStruct(shape, dtype) for...]
  transfers between devices with their start and end apart: 3 -> 2, of which waited for: 1 -> 0; matrix products, arithmetic and copies ran while one was open for 0% -> 0% of each run, Pallas kernels for 6% -> 3%
where the time goes in v6:
time: 57.6 us; the launch traced here: 57.4 us
  blocking collectives  39.1 us (68%)
  starting transfers between devices  9.45 us (16%)
  Pallas kernels  8.14 us (14%)
  between operations  0.71 us (1%)
    all_to_all x3, blocking collectives, exchange(): lax.all_to_all(cut, axes, 0, 0, axis_index_groups=groups)  39.1 us
    pallas_call x8, Pallas kernels, call(): pl.pallas_call(kernel, out_shape=[jax.ShapeDtypeStruct(shape, dtype) for...  8.14 us
    ppermute x1, starting transfers between devices, shards(): from_core = lax.ppermute(to_core, 'core', [(0, 1), (1, 0)])  4.94 us
    ppermute x1, starting transfers between devices, shards(): lax.ppermute(to_chip, BLOCKS, pairs + [(j, i) for i, j in pairs])  4.51 us
  transfers between devices with their start and end apart: 2, of which 0 were waited for; matrix products, arithmetic and copies ran while one was open for 0% of the time, Pallas kernels for 3%

profile of v6, /device:TPU:1, one launch (start us, length us, event | category | flops | bytes accessed | tf_op | source)
XLA Modules:
  0.0 57.4 jit_solution(10209980678874283968)
XLA Ops:
  0.6 1.2 %pack.1 = (bf16[8,2560]{1,0:T(8,128)(2,1)S(1)}, bf16[8,2560]{1,0:T(8,128)(2,1)S(1)}, bf16[128,256]{1,0:T(8,128)(2,1)S(1)}, f32[8,256]{1,0:T(8,128)S(1)}, bf16[8,...) custom-call(s32[1,8]{1,0:T(1,128)} %active.1, bf16[8,16384]{1,0:T(8,128)(2,1)} %bitcast.16, ...), custom_call_target="tpu_custom_call" | custom-call | tf_op jit(solution)/shard_map/pack/pallas_call | solution.py:406
  1.8 4.5 %collective-permute-start = (bf16[8,2560]{1,0:T(8,128)(2,1)S(1)}, bf16[8,2560]{1,0:T(8,128)(2,1)S(1)}, u32[]{:S(2)}, u32[]{:S(2)}) collective-permute-start(bf16[8,2560]{1,0:T(8,128)(2,1)S(1)} %get-tuple-element.34), channel_id=1, source_target_pairs={{4,8},{12,16},{20,24},{28,32},{36,40},{44,48},{52,56},{60,64},{68,... | collective-permute-start | bytes 122888 | tf_op jit(solution)/shard_map/ppermute | solution.py:449
  6.4 4.9 %collective-permute-start.1 = (bf16[8,2560]{1,0:T(8,128)(2,1)S(1)}, bf16[8,2560]{1,0:T(8,128)(2,1)S(1)}, u32[]{:S(2)}, u32[]{:S(2)}) collective-permute-start(bf16[8,2560]{1,0:T(8,128)(2,1)S(1)} %get-tuple-element.35), channel_id=1, source_target_pairs={{0,4},{4,0},{1,5},{5,1},{2,6},{6,2},{3,7},{7,3},{8,12},{12,8},{9,1... | collective-permute-start | bytes 122888 | tf_op jit(solution)/shard_map/ppermute | solution.py:450
  11.3 1.8 %inner.1 = (bf16[8,80,640]{2,1,0:T(8,128)(2,1)S(1)}, bf16[8,64,640]{2,1,0:T(8,128)(2,1)S(1)}, bf16[9,384,256]{2,1,0:T(8,128)(2,1)S(1)}, bf16[256,1024]{1,0:T(8,1...) custom-call(f32[8,256]{1,0:T(8,128)S(1)} %get-tuple-element.27.live_in.re, ...), custom_call_target="tpu_custom_call" | custom-call | tf_op jit(solution)/shard_map/inner/pallas_call | solution.py:406
  13.1 0.0 collective-permute-done.refs_2_
  13.2 0.0 collective-permute-done.1.refs_3_
  13.2 1.9 %main.1 = (bf16[384,128]{1,0:T(8,128)(2,1)S(1)}, bf16[10,64,256]{2,1,0:T(8,128)(2,1)S(1)}) custom-call(bf16[8,64,640]{2,1,0:T(8,128)(2,1)S(1)} %get-tuple-element.32.refs_0_, bf16[8,80,640]{2,1,0:T(8,128)(2,1)S(1)} %get-tuple-element.33.refs_1_, bf16[8,2560]{1,0:T(8,128)(2,1)S(1)} %collective-permute-done.refs_2_, ...), custom_call_target="tpu_custom_call" | custom-call | tf_op jit(solution)/shard_map/main/pallas_call | solution.py:406
  15.1 9.2 %all_to_all.15 = bf16[32,3,4,128]{3,2,1,0:T(4,128)(2,1)S(1)} all-to-all(bf16[32,3,4,128]{3,2,1,0:T(4,128)(2,1)S(1)} %bitcast.14), channel_id=1, replica_groups={{22,23,20,21,18,19,16,17,30,31,28,29,26,27,24,25,6,7,4,5,2,3,0,1,14,15,..., dimensions={0} | all-to-all | bytes 196608 | tf_op jit(solution)/shard_map/all_to_all | solution.py:400
  24.3 2.2 %back0.1.refs_0_ = bf16[8,16384]{1,0:T(8,128)(2,1)} custom-call(f32[8,256]{1,0:T(8,128)S(1)} %get-tuple-element.27.live_in.refs_0_.refs_1_, bf16[27,32,32]{2,1,0:T(8,128)(2,1)S(1)} %get-tuple-element.29.conv.refs_1_.refs_2_, bf16[10,64,256]{2,1,0:T(8,128)(2,1)S(1)} %get-tuple-element.44.refs_2_.refs_3_, ...), custom_call_target="tpu_custom_call" | custom-call | tf_op jit(solution)/shard_map/back0/pallas_call | solution.py:406
  26.5 18.2 %all_to_all.16 = bf16[16,3,4,128]{3,2,1,0:T(4,128)(2,1)S(1)} all-to-all(bf16[16,3,4,128]{3,2,1,0:T(4,128)(2,1)S(1)} %bitcast.12), channel_id=1, replica_groups={{256,288,320,352,384,416,448,480,0,32,64,96,128,160,192,224},{257,289,3..., dimensions={0} | all-to-all | bytes 98304 | tf_op jit(solution)/shard_map/all_to_all | solution.py:400
  44.7 11.7 %all_to_all.17 = bf16[32,3,4,128]{3,2,1,0:T(4,128)(2,1)S(1)} all-to-all(bf16[32,3,4,128]{3,2,1,0:T(4,128)(2,1)S(1)} %bitcast.11), channel_id=1, replica_groups={{22,23,20,21,18,19,16,17,30,31,28,29,26,27,24,25,6,7,4,5,2,3,0,1,14,15,..., dimensions={0} | all-to-all | bytes 196608 | tf_op jit(solution)/shard_map/all_to_all | solution.py:400
  56.4 1.0 %finish.1 = (f32[27,32,32]{2,1,0:T(8,128)}, f32[8,32,64]{2,1,0:T(8,128)}) custom-call(bf16[384,128]{1,0:T(8,128)(2,1)S(1)} %bitcast.9), custom_call_target="tpu_custom_call" | custom-call | tf_op jit(solution)/shard_map/finish/pallas_call | solution.py:406
  (3 shorter events, 0.1 us)
Async XLA Ops:
  1.8 11.3 %collective-permute-start = (bf16[8,2560]{1,0:T(8,128)(2,1)S(1)}, bf16[8,2560]{1,0:T(8,128)(2,1)S(1)}, u32[]{:S(2)}, u32[]{:S(2)}) collective-permute-start(bf16[8,2560]{1,0:T(8,128)(2,1)S(1)} %get-tuple-element.34), channel_id=1, source_target_pairs={{4,8},{12,16},{20,24},{28,32},{36,40},{44,48},{52,56},{60,64},{68,... | collective-permute-start | bytes 122888 | tf_op jit(solution)/shard_map/ppermute | solution.py:449
  6.4 6.8 %collective-permute-start.1 = (bf16[8,2560]{1,0:T(8,128)(2,1)S(1)}, bf16[8,2560]{1,0:T(8,128)(2,1)S(1)}, u32[]{:S(2)}, u32[]{:S(2)}) collective-permute-start(bf16[8,2560]{1,0:T(8,128)(2,1)S(1)} %get-tuple-element.35), channel_id=1, source_target_pairs={{0,4},{4,0},{1,5},{5,1},{2,6},{6,2},{3,7},{7,3},{8,12},{12,8},{9,1... | collective-permute-start | bytes 122888 | tf_op jit(solution)/shard_map/ppermute | solution.py:450

commit v7 on v6

--- a/solution.py
+++ b/solution.py
@@ -17,6 +17,7 @@
 
 ROW = 256
 WIDE = 384
+TAPS = 1024
 GRADS = 384
 SENT = BF16
 
@@ -59,8 +60,12 @@
     ring = [low] + full + [high]
     for k in range(5):
         outer[z, 16 * k : 16 * k + 16] = jnp.concatenate(ring[2 * k : 2 * k + 2], 0).astype(BF16)
+    tile = slice(ROW, WIDE)
+    edges = [ring[y][:, tile] + pltpu.roll(ring[y + 1][:, tile], 64, 1) for y in range(8)]
+    both = [jnp.concatenate([row[:, :ROW], edge, row[:, WIDE:]], 1) if halves
+            else jnp.concatenate([row[:, :ROW], edge], 1) for row, edge in zip(full, edges)]
     for k in range(4):
-        inner[z, 16 * k : 16 * k + 16] = jnp.concatenate(full[2 * k : 2 * k + 2], 0).astype(BF16)
+        inner[z, 16 * k : 16 * k + 16] = jnp.concatenate(both[2 * k : 2 * k + 2], 0).astype(BF16)
 
 
 def window(outer, inner, first, count, oz, oy, lanes):
@@ -72,10 +77,11 @@
 
 def convolve(outer, inner, bands, first, count):
     left = [
-        window(outer, inner, first, count, index // 3, index % 3, slice(0, WIDE)) for index in range(9)
+        window(outer, inner, first, count, index // 3, index % 3, slice(0, WIDE if index % 3 else ROW))
+        for index in range(9)
     ]
     return jnp.dot(
-        jnp.concatenate(left, 1), bands[...].reshape(9 * WIDE, ROW), preferred_element_type=F32
+        jnp.concatenate(left, 1), bands[...].reshape(3 * TAPS, ROW), preferred_element_type=F32
     )
 
 
@@ -95,14 +101,19 @@
 
 def put_bands(bands, index, taps):
     spot = iota((32, ROW), 1) // 32
+    oz, oy = index // 3, index % 3
+    start = (0, ROW, ROW + WIDE)[oy]
     for i in range(8):
         part = jnp.zeros((32, ROW), F32)
         for ox in range(3):
             part = jnp.where(spot == i + 1 - ox, taps[ox], part)
-        bands[index, 32 * i : 32 * i + 32] = part.astype(BF16)
-    bands[index, 256:288] = jnp.where(spot == 7, taps[2], 0.0).astype(BF16)
-    bands[index, 288:352] = jnp.zeros((64, ROW), BF16)
-    bands[index, 352:384] = jnp.where(spot == 0, taps[0], 0.0).astype(BF16)
+        bands[oz, start + 32 * i : start + 32 * i + 32] = part.astype(BF16)
+    edge = 2 * ROW if oy < 2 else TAPS - 128
+    right, left = (64, 32) if oy == 1 else (0, 96)
+    bands[oz, edge + right : edge + right + 32] = jnp.where(spot == 7, taps[2], 0.0).astype(BF16)
+    bands[oz, edge + left : edge + left + 32] = jnp.where(spot == 0, taps[0], 0.0).astype(BF16)
+    if oy == 2:
+        bands[oz, edge + 32 : edge + 96] = jnp.zeros((64, ROW), BF16)
 
 
 def pack_kernel(
@@ -451,7 +462,7 @@
     outer, inner, bands, spread, dpre, dy, state = call(
         inner_kernel,
         [
-            ((8, 80, full), BF16), ((8, 64, full), BF16), ((9, WIDE, ROW), BF16), ((ROW, 4 * ROW), BF16),
+            ((8, 80, full), BF16), ((8, 64, full), BF16), ((3, TAPS, ROW), BF16), ((ROW, 4 * ROW), BF16),
             ((6, 64, ROW), BF16), ((8, 64, ROW), F32), ((4, 128, ROW), BF16),
         ],
         [live, fine, conv, down, coarse],
@@ -477,7 +488,7 @@
             functools.partial(back_turn, turn), [((8, 64 * ROW), BF16)], arrays + [live, conv, dpre, dy],
             [
                 pltpu.VMEM((8, 64 * ROW), BF16), pltpu.VMEM((10, 80, WIDE), BF16),
-                pltpu.VMEM((10, 64, WIDE), BF16), pltpu.VMEM((9, WIDE, ROW), BF16),
+                pltpu.VMEM((10, 64, WIDE), BF16), pltpu.VMEM((3, TAPS, ROW), BF16),
                 pltpu.SemaphoreType.DMA((1,)),
             ],
             far=turn, out_space=pltpu.HBM, same=[(0, 0)] * turn, name=f"back{turn}",

time: 57.6 us -> 57.5 us (level)
  no operation moved by 1% of the time
where the time goes in v7:
time: 57.5 us; the launch traced here: 57.2 us
  blocking collectives  39.2 us (68%)
  starting transfers between devices  9.45 us (16%)
  Pallas kernels  7.85 us (14%)
  between operations  0.71 us (1%)
    all_to_all x3, blocking collectives, exchange(): lax.all_to_all(cut, axes, 0, 0, axis_index_groups=groups)  39.2 us
    pallas_call x8, Pallas kernels, call(): pl.pallas_call(kernel, out_shape=[jax.ShapeDtypeStruct(shape, dtype) for...  7.85 us
    ppermute x1, starting transfers between devices, shards(): from_core = lax.ppermute(to_core, 'core', [(0, 1), (1, 0)])  4.94 us
    ppermute x1, starting transfers between devices, shards(): lax.ppermute(to_chip, BLOCKS, pairs + [(j, i) for i, j in pairs])  4.51 us
  transfers between devices with their start and end apart: 2, of which 0 were waited for; matrix products, arithmetic and copies ran while one was open for 0% of the time, Pallas kernels for 3%

profile of v7, /device:TPU:1, one launch (start us, length us, event | category | flops | bytes accessed | tf_op | source)
XLA Modules:
  0.0 57.2 jit_solution(8691178222732267502)
XLA Ops:
  0.6 1.2 %pack.1 = (bf16[8,2560]{1,0:T(8,128)(2,1)S(1)}, bf16[8,2560]{1,0:T(8,128)(2,1)S(1)}, bf16[128,256]{1,0:T(8,128)(2,1)S(1)}, f32[8,256]{1,0:T(8,128)S(1)}, bf16[8,...) custom-call(s32[1,8]{1,0:T(1,128)} %active.1, bf16[8,16384]{1,0:T(8,128)(2,1)} %bitcast.16, ...), custom_call_target="tpu_custom_call" | custom-call | tf_op jit(solution)/shard_map/pack/pallas_call | solution.py:417
  1.8 4.5 %collective-permute-start = (bf16[8,2560]{1,0:T(8,128)(2,1)S(1)}, bf16[8,2560]{1,0:T(8,128)(2,1)S(1)}, u32[]{:S(2)}, u32[]{:S(2)}) collective-permute-start(bf16[8,2560]{1,0:T(8,128)(2,1)S(1)} %get-tuple-element.34), channel_id=1, source_target_pairs={{4,8},{12,16},{20,24},{28,32},{36,40},{44,48},{52,56},{60,64},{68,... | collective-permute-start | bytes 122888 | tf_op jit(solution)/shard_map/ppermute | solution.py:460
  6.4 4.9 %collective-permute-start.1 = (bf16[8,2560]{1,0:T(8,128)(2,1)S(1)}, bf16[8,2560]{1,0:T(8,128)(2,1)S(1)}, u32[]{:S(2)}, u32[]{:S(2)}) collective-permute-start(bf16[8,2560]{1,0:T(8,128)(2,1)S(1)} %get-tuple-element.35), channel_id=1, source_target_pairs={{0,4},{4,0},{1,5},{5,1},{2,6},{6,2},{3,7},{7,3},{8,12},{12,8},{9,1... | collective-permute-start | bytes 122888 | tf_op jit(solution)/shard_map/ppermute | solution.py:461
  11.3 1.8 %inner.1 = (bf16[8,80,640]{2,1,0:T(8,128)(2,1)S(1)}, bf16[8,64,640]{2,1,0:T(8,128)(2,1)S(1)}, bf16[3,1024,256]{2,1,0:T(8,128)(2,1)S(1)}, bf16[256,1024]{1,0:T(8,...) custom-call(f32[8,256]{1,0:T(8,128)S(1)} %get-tuple-element.27.live_in.r, ...), custom_call_target="tpu_custom_call" | custom-call | tf_op jit(solution)/shard_map/inner/pallas_call | solution.py:417
  13.1 0.0 collective-permute-done.refs_2_
  13.1 0.0 collective-permute-done.1.refs_3_
  13.1 1.8 %main.1 = (bf16[384,128]{1,0:T(8,128)(2,1)S(1)}, bf16[10,64,256]{2,1,0:T(8,128)(2,1)S(1)}) custom-call(bf16[8,64,640]{2,1,0:T(8,128)(2,1)S(1)} %get-tuple-element.32.refs_0_, bf16[8,80,640]{2,1,0:T(8,128)(2,1)S(1)} %get-tuple-element.33.refs_1_, bf16[8,2560]{1,0:T(8,128)(2,1)S(1)} %collective-permute-done.refs_2_, ...), custom_call_target="tpu_custom_call" | custom-call | tf_op jit(solution)/shard_map/main/pallas_call | solution.py:417
  14.9 9.2 %all_to_all.15 = bf16[32,3,4,128]{3,2,1,0:T(4,128)(2,1)S(1)} all-to-all(bf16[32,3,4,128]{3,2,1,0:T(4,128)(2,1)S(1)} %bitcast.14), channel_id=1, replica_groups={{22,23,20,21,18,19,16,17,30,31,28,29,26,27,24,25,6,7,4,5,2,3,0,1,14,15,..., dimensions={0} | all-to-all | bytes 196608 | tf_op jit(solution)/shard_map/all_to_all | solution.py:411
  24.2 2.1 %back0.1.refs_0_ = bf16[8,16384]{1,0:T(8,128)(2,1)} custom-call(f32[8,256]{1,0:T(8,128)S(1)} %get-tuple-element.27.live_in.refs_0_.refs_1_, bf16[27,32,32]{2,1,0:T(8,128)(2,1)S(1)} %get-tuple-element.29.conv.refs_1_.refs_2_, bf16[10,64,256]{2,1,0:T(8,128)(2,1)S(1)} %get-tuple-element.44.refs_2_.refs_3_, ...), custom_call_target="tpu_custom_call" | custom-call | tf_op jit(solution)/shard_map/back0/pallas_call | solution.py:417
  26.2 18.3 %all_to_all.16 = bf16[16,3,4,128]{3,2,1,0:T(4,128)(2,1)S(1)} all-to-all(bf16[16,3,4,128]{3,2,1,0:T(4,128)(2,1)S(1)} %bitcast.12), channel_id=1, replica_groups={{256,288,320,352,384,416,448,480,0,32,64,96,128,160,192,224},{257,289,3..., dimensions={0} | all-to-all | bytes 98304 | tf_op jit(solution)/shard_map/all_to_all | solution.py:411
  44.6 11.7 %all_to_all.17 = bf16[32,3,4,128]{3,2,1,0:T(4,128)(2,1)S(1)} all-to-all(bf16[32,3,4,128]{3,2,1,0:T(4,128)(2,1)S(1)} %bitcast.11), channel_id=1, replica_groups={{22,23,20,21,18,19,16,17,30,31,28,29,26,27,24,25,6,7,4,5,2,3,0,1,14,15,..., dimensions={0} | all-to-all | bytes 196608 | tf_op jit(solution)/shard_map/all_to_all | solution.py:411
  56.2 1.0 %finish.1 = (f32[27,32,32]{2,1,0:T(8,128)}, f32[8,32,64]{2,1,0:T(8,128)}) custom-call(bf16[384,128]{1,0:T(8,128)(2,1)S(1)} %bitcast.9), custom_call_target="tpu_custom_call" | custom-call | tf_op jit(solution)/shard_map/finish/pallas_call | solution.py:417
  (3 shorter events, 0.1 us)
Async XLA Ops:
  1.8 11.2 %collective-permute-start = (bf16[8,2560]{1,0:T(8,128)(2,1)S(1)}, bf16[8,2560]{1,0:T(8,128)(2,1)S(1)}, u32[]{:S(2)}, u32[]{:S(2)}) collective-permute-start(bf16[8,2560]{1,0:T(8,128)(2,1)S(1)} %get-tuple-element.34), channel_id=1, source_target_pairs={{4,8},{12,16},{20,24},{28,32},{36,40},{44,48},{52,56},{60,64},{68,... | collective-permute-start | bytes 122888 | tf_op jit(solution)/shard_map/ppermute | solution.py:460
  6.4 6.7 %collective-permute-start.1 = (bf16[8,2560]{1,0:T(8,128)(2,1)S(1)}, bf16[8,2560]{1,0:T(8,128)(2,1)S(1)}, u32[]{:S(2)}, u32[]{:S(2)}) collective-permute-start(bf16[8,2560]{1,0:T(8,128)(2,1)S(1)} %get-tuple-element.35), channel_id=1, source_target_pairs={{0,4},{4,0},{1,5},{5,1},{2,6},{6,2},{3,7},{7,3},{8,12},{12,8},{9,1... | collective-permute-start | bytes 122888 | tf_op jit(solution)/shard_map/ppermute | solution.py:461
